TPU v7x, 32 devices: a whole 2x2x4 slice. The times are simulated.
32 devices in a mesh: gx: 4 (over y, core), gy: 4 (over z), gz: 2 (over x).
Axes of the slice: x: 2, y: 2, z: 4, core: 2. Of those that a mesh axis runs over, the one named last changes fastest.
Arguments:
- particles: float32 [26, 16384], P(None, ('gx', 'gy', 'gz')), may hold values from -4 to 4, as said below
- block_ids: int32 [16384], P(('gx', 'gy', 'gz')), may hold values from 0 to 7
- node_offsets: int32 [16384], P(('gx', 'gy', 'gz')), may hold values from 0 to 511
- live_count: int32 [32], P(('gx', 'gy', 'gz')), may hold values from 64 to 512, as said below
- migrations: int32 [6, 256], P(None, ('gx', 'gy', 'gz')), may hold values from 0 to 511, as said below
Outputs:
- moved_records: float32 [26, 16384], P(None, ('gx', 'gy', 'gz'))
Inputs may be any that keep to these rules, and one draw needn't show every extreme that they name: `live_count`: slots below a domain's count are live; some domain is full and some holds exactly 64. `migrations`: the 48 entries of one domain are distinct slots, each live in that domain. `particles`: entries of F lie within 0.15 of the identity's; positions within a cell between -0.5 and 0.5; masses between 0.5 and 2; plastic ratios between 0.9 and 1.1.
All inputs are finite; a program needn't handle non-finite values.
Results may differ from a plain program's by a relative error of at most 0.0003.
Values sent between devices are 32-bit elements; how exact they have to be, the bound alone decides.
A program may use at most 64 MiB of HBM per device.

v0:
```python
import jax
import jax.numpy as jnp
from jax import lax
from jax.sharding import PartitionSpec as P

BLK = 2


time_step = 0.05
stress_gain = 0.2
shear_zero = 5.0
bulk_zero = 5.0
harden_rate = 10.0
mass_floor = 0.1
gravity = 9.8
highest = lax.Precision.HIGHEST


def extended_2(block, sides, width):
    for axis, dim in sides:
        count = lax.axis_size(axis)
        forward = [(i, i + 1) for i in range(count - 1)]
        forward.append((count - 1, 0))
        backward = [(target, source) for source, target in forward]
        low = lax.ppermute(
            lax.slice_in_dim(block, block.shape[dim] - width, None, axis=dim), axis, forward
        )
        high = lax.ppermute(lax.slice_in_dim(block, 0, width, axis=dim), axis, backward)
        block = jnp.concatenate([low, block, high], axis=dim)
    return block


def matrix_product(left_side, right_side):
    rows_out = []
    for row_id in range(3):
        entries = []
        for col_id in range(3):
            entries.append(
                left_side[row_id, 0] * right_side[0, col_id]
                + left_side[row_id, 1] * right_side[1, col_id]
                + left_side[row_id, 2] * right_side[2, col_id]
            )
        rows_out.append(jnp.stack(entries))
    return jnp.stack(rows_out)


def matrix_vector(matrix, vector):
    return jnp.stack(
        [
            matrix[row_id, 0] * vector[0]
            + matrix[row_id, 1] * vector[1]
            + matrix[row_id, 2] * vector[2]
            for row_id in range(3)
        ]
    )


def matrix_transpose(matrix):
    return jnp.transpose(matrix, (1, 0, 2))


def determinant(matrix):
    return (
        matrix[0, 0] * (matrix[1, 1] * matrix[2, 2] - matrix[1, 2] * matrix[2, 1])
        - matrix[0, 1] * (matrix[1, 0] * matrix[2, 2] - matrix[1, 2] * matrix[2, 0])
        + matrix[0, 2] * (matrix[1, 0] * matrix[2, 1] - matrix[1, 1] * matrix[2, 0])
    )


def kirchhoff(deform, plastic):
    identity = jnp.eye(3, dtype=deform.dtype)[:, :, None]
    rotation = deform
    for iteration in range(5):
        rotation = 0.5 * matrix_product(
            rotation, 3.0 * identity - matrix_product(matrix_transpose(rotation), rotation)
        )
    volume = determinant(deform)
    harden = jnp.exp(harden_rate * (1.0 - plastic))
    shear_mod = shear_zero * harden
    bulk_mod = bulk_zero * harden
    return (
        2.0 * shear_mod * matrix_product(deform - rotation, matrix_transpose(deform))
        + bulk_mod * (volume - 1.0) * volume * identity
    )


def spline_weights(fraction):
    return jnp.stack(
        [0.5 * (0.5 - fraction) ** 2, 0.75 - fraction * fraction, 0.5 * (0.5 + fraction) ** 2]
    )


def anchor_nodes(block_ids, node_offsets, blocks):
    corner = jnp.stack(
        [block_ids // (blocks * blocks), block_ids // blocks % blocks, block_ids % blocks]
    )
    inside = jnp.stack([node_offsets // 64, node_offsets // 8 % 8, node_offsets % 8])
    return 8 * corner + inside + 8


def axis_tables(anchor_line, weight_line, node_span):
    coords = jnp.arange(node_span, dtype=jnp.int32)[:, None]
    lower = (coords == anchor_line[None, :] - 1).astype(jnp.float32)
    centre = (coords == anchor_line[None, :]).astype(jnp.float32)
    upper = (coords == anchor_line[None, :] + 1).astype(jnp.float32)
    weighted = (
        weight_line[0][None, :] * lower
        + weight_line[1][None, :] * centre
        + weight_line[2][None, :] * upper
    )
    shifted = weight_line[2][None, :] * upper - weight_line[0][None, :] * lower
    return (weighted, shifted)


def outer_rows(first, second):
    return (first[:, None, :] * second[None, :, :]).reshape(-1, first.shape[1])


def contract_last(left_side, right_side):
    return lax.dot_general(
        left_side,
        right_side,
        (((1,), (1,)), ((), ())),
        precision=highest,
        preferred_element_type=jnp.float32,
    )


def contract_inner(left_side, right_side):
    return lax.dot_general(
        left_side,
        right_side,
        (((1,), (0,)), ((), ())),
        precision=highest,
        preferred_element_type=jnp.float32,
    )


def block_width(count):
    return min(512, count)


def node_to_block(nodes, blocks):
    channels = nodes.shape[0]
    padded = blocks + 2
    split = nodes.reshape(channels, padded, 8, padded, 8, padded, 8).transpose(0, 1, 3, 5, 2, 4, 6)
    return split.reshape(channels, padded, padded, padded, 512)


def block_to_node(grid, blocks):
    channels = grid.shape[0]
    padded = blocks + 2
    split = grid.reshape(channels, padded, padded, padded, 8, 8, 8).transpose(0, 1, 4, 2, 5, 3, 6)
    return split.reshape(channels, 8 * padded, 8 * padded, 8 * padded)


def particle_tables(fraction, anchor, node_span):
    weights_axis = spline_weights(fraction)
    tables = [
        axis_tables(anchor[axis_id], weights_axis[:, axis_id], node_span) for axis_id in range(3)
    ]
    return tables


def scatter_grid(particles, block_ids, node_offsets, living, blocks):
    node_span = 8 * (blocks + 2)
    fraction = particles[21:24]
    affine = particles[3:12].reshape(3, 3, -1)
    deform = particles[12:21].reshape(3, 3, -1)
    particle_mass = particles[24] * living
    coupling = (particles[24] * affine - stress_gain * kirchhoff(deform, particles[25])) * living
    momentum = particle_mass * particles[0:3]
    anchor = anchor_nodes(block_ids, node_offsets, blocks)
    base_terms = jnp.concatenate(
        [particle_mass[None], momentum - matrix_vector(coupling, fraction)]
    )
    tables = particle_tables(fraction, anchor, node_span)
    weight_x = tables[0][0]
    shift_x = tables[0][1]
    weight_y = tables[1][0]
    shift_y = tables[1][1]
    weight_z = tables[2][0]
    shift_z = tables[2][1]
    left_first = jnp.concatenate(
        [outer_rows(base_terms, weight_x), outer_rows(coupling[:, 0], shift_x)]
    )
    first_sum = contract_last(left_first, outer_rows(weight_y, weight_z))
    second_sum = contract_last(outer_rows(coupling[:, 1], weight_x), outer_rows(shift_y, weight_z))
    third_sum = contract_last(outer_rows(coupling[:, 2], weight_x), outer_rows(weight_y, shift_z))
    base_total = first_sum[: 4 * node_span]
    push_total = first_sum[4 * node_span :] + second_sum + third_sum
    nodes = base_total.reshape(4, node_span, node_span, node_span)
    nodes = nodes.at[1:4].add(push_total.reshape(3, node_span, node_span, node_span))
    return node_to_block(nodes, blocks)


def grid_update(totals):
    velocity = totals[1:4] / jnp.maximum(totals[0:1], mass_floor)
    return velocity.at[2].add(-time_step * gravity)


def gather_grid(particles, block_ids, node_offsets, living, blocks, velocity_grid):
    node_span = 8 * (blocks + 2)
    count = particles.shape[1]
    fraction = particles[21:24]
    deform = particles[12:21].reshape(3, 3, -1)
    anchor = anchor_nodes(block_ids, node_offsets, blocks)
    tables = particle_tables(fraction, anchor, node_span)
    velocity_nodes = block_to_node(velocity_grid, blocks).reshape(
        3 * node_span, node_span * node_span
    )
    width = block_width(count)
    weight_x = tables[0][0]
    shift_x = tables[0][1]
    weight_y = tables[1][0]
    shift_y = tables[1][1]
    weight_z = tables[2][0]
    shift_z = tables[2][1]
    first_read = contract_inner(velocity_nodes, outer_rows(weight_y, weight_z)).reshape(
        3, node_span, width
    )
    second_read = contract_inner(velocity_nodes, outer_rows(shift_y, weight_z)).reshape(
        3, node_span, width
    )
    third_read = contract_inner(velocity_nodes, outer_rows(weight_y, shift_z)).reshape(
        3, node_span, width
    )
    velocity_parts = jnp.sum(weight_x[None] * first_read, axis=1)
    along_parts = jnp.stack(
        [
            jnp.sum(shift_x[None] * first_read, axis=1),
            jnp.sum(weight_x[None] * second_read, axis=1),
            jnp.sum(weight_x[None] * third_read, axis=1),
        ],
        axis=1,
    )
    new_affine = 4.0 * (along_parts - velocity_parts[:, None, :] * fraction[None, :, :])
    new_deform = deform + time_step * matrix_product(new_affine, deform)
    new_fraction = fraction + time_step * velocity_parts
    record_rows = jnp.concatenate(
        [
            velocity_parts,
            new_affine.reshape(9, -1),
            new_deform.reshape(9, -1),
            new_fraction,
            particles[24:26],
        ]
    )
    return record_rows * living


def fold_narrow(extended, along, blocks):
    centre = lax.slice_in_dim(extended, 2, blocks + 2, axis=along)
    lower_side = lax.slice_in_dim(extended, 0, 1, axis=along)
    upper_side = lax.slice_in_dim(extended, blocks + 3, blocks + 4, axis=along)
    first_block = lax.slice_in_dim(centre, 0, 1, axis=along) + lower_side
    middle = lax.slice_in_dim(centre, 1, blocks - 1, axis=along)
    last_block = lax.slice_in_dim(centre, blocks - 1, blocks, axis=along) + upper_side
    return jnp.concatenate([first_block, middle, last_block], axis=along)


def node_window(grid, blocks):
    nodes = block_to_node(grid, blocks)
    return nodes[:, 7 : 8 * blocks + 9, 7 : 8 * blocks + 9, 7 : 8 * blocks + 9]


def block_layout(nodes, blocks):
    filled = jnp.pad(nodes, ((0, 0), (7, 7), (7, 7), (7, 7)))
    return node_to_block(filled, blocks)


def body(particles, block_ids, node_offsets, live_count, migrations):
    slot_index = jnp.arange(particles.shape[1], dtype=jnp.int32)
    living = (slot_index < live_count[0]).astype(particles.dtype)
    grid_sums = scatter_grid(particles, block_ids, node_offsets, living, BLK)
    node_sums = node_window(grid_sums, BLK)
    node_extended = extended_2(node_sums, (("gx", 1), ("gy", 2), ("gz", 3)), 1)
    node_span = 8 * BLK
    node_totals = fold_narrow(
        fold_narrow(fold_narrow(node_extended, 1, node_span), 2, node_span), 3, node_span
    )
    node_velocity = grid_update(node_totals)
    read_nodes = extended_2(node_velocity, (("gx", 1), ("gy", 2), ("gz", 3)), 1)
    velocity_grid = block_layout(read_nodes, BLK)
    updated = gather_grid(particles, block_ids, node_offsets, living, BLK, velocity_grid)
    chosen = migrations.reshape(-1)
    selector = (chosen[:, None] == slot_index[None, :]).astype(jnp.float32)
    outgoing = contract_last(updated, selector).reshape(26, 6, -1)
    toward_first = jnp.stack([outgoing[:, 1], outgoing[:, 0]])
    toward_second = jnp.stack([outgoing[:, 3], outgoing[:, 2]])
    toward_third = jnp.stack([outgoing[:, 5], outgoing[:, 4]])
    arrive_first = extended_2(toward_first, (("gx", 0),), 1)
    arrive_second = extended_2(toward_second, (("gy", 0),), 1)
    arrive_third = extended_2(toward_third, (("gz", 0),), 1)
    arrived = jnp.stack(
        [
            arrive_first[0],
            arrive_first[3],
            arrive_second[0],
            arrive_second[3],
            arrive_third[0],
            arrive_third[3],
        ],
        axis=1,
    )
    taken = jnp.sum(selector, axis=0)
    placed = contract_inner(arrived.reshape(26, -1), selector)
    return updated * (1.0 - taken)[None, :] + placed


def solution(mesh):
    return jax.shard_map(
        body,
        mesh=mesh,
        in_specs=(
            P(None, ("gx", "gy", "gz")),
            P(("gx", "gy", "gz")),
            P(("gx", "gy", "gz")),
            P(("gx", "gy", "gz")),
            P(None, ("gx", "gy", "gz")),
        ),
        out_specs=P(None, ("gx", "gy", "gz")),
        check_vma=False,
    )
```

profile of v0, /device:TPU:0, one launch (start us, length us, event | category | flops | bytes accessed | tf_op | source)
XLA Modules:
  0.0 80.1 jit_solution(13076377914251529244)
XLA Ops:
  0.0 0.9 %fusion.80 = (f32[9,512]{1,0:T(8,128)S(1)}, f32[9,512]{1,0:T(8,128)S(1)}) fusion(f32[26,512]{1,0:T(8,128)} %param.9), kind=kLoop, calls=%fused_computation.376 | loop fusion | bytes 73728 | tf_op jit(solution)/shard_map/slice | solution.py:168
  5.0 0.8 %broadcast_multiply_fusion = (f32[32,32,512]{2,1,0:T(8,128)S(1)}, f32[32,32,512]{2,1,0:T(8,128)S(1)}, f32[32,32,512]{2,1,0:T(8,128)S(1)}) fusion(f32[32,512]{1,0:T(8,128)S(1)} %get-tuple-element.185, f32[32,512]{1,0:T(8,128)S(1)} %get-tuple-element.188, f32[32,512]{1,0:T(8,128)S(1)} %get-tuple-element.186, f32[32,512]{1,0:T(8,128)S(1)} %get-tuple-element.187), kind=kLoop, calls=%fused_computation.36 | loop fusion | flops 1572864 | bytes 6553600 | tf_op jit(solution)/shard_map/mul | solution.py:116
  5.8 2.1 %fusion.33 = f32[224,1024]{1,0:T(8,128)S(1)} fusion(f32[1024,512]{1,0:T(8,128)S(1)} %bitcast.571, f32[96,512]{1,0:T(8,128)S(1)} %bitcast.574, f32[128,512]{1,0:T(8,128)S(1)} %bitcast.572), kind=kOutput, calls=%fused_computation.47 | convolution fusion | flops 1409400832 | bytes 3473408 | tf_op jit(solution)/shard_map/dot_general | solution.py:120
  8.0 2.2 %convolution_add_fusion.1 = f32[96,1024]{1,0:T(8,128)S(1)} fusion(f32[96,512]{1,0:T(8,128)S(1)} %bitcast.573, f32[1024,512]{1,0:T(8,128)S(1)} %bitcast.570, f32[224,1024]{1,0:T(8,128)S(1)} %fusion.33), kind=kOutput, calls=%fused_computation.25 | convolution fusion | flops 604078080 | bytes 3080192 | tf_op jit(solution)/shard_map/dot_general | solution.py:120
  10.1 2.2 %fusion.11 = f32[96,1024]{1,0:T(8,128)S(1)} fusion(f32[96,1024]{1,0:T(8,128)S(1)} %convolution_add_fusion.1, f32[96,512]{1,0:T(8,128)S(1)} %bitcast.575, f32[1024,512]{1,0:T(8,128)S(1)} %bitcast.569, f32[224,1024]{1,0:T(8,128)S(1)} %fusion.33), kind=kOutput, calls=%fused_computation.26 | convolution fusion | flops 604176384 | bytes 3473408 | tf_op jit(solution)/shard_map/dot_general | solution.py:120
  12.3 1.7 %add.3113 = f32[3,32,32,32]{3,2,1,0:T(8,128)} reshape(f32[96,1024]{1,0:T(8,128)S(1)} %fusion.11) | data formatting | bytes 786432 | tf_op jit(solution)/shard_map/add | solution.py:193
  14.0 0.7 reshape.7526
  14.7 1.2 %copy.98 = f32[4,32,32,32]{3,1,2,0:T(8,128)S(1)} copy(f32[4,32,32,32]{3,2,1,0:T(8,128)S(1)} %reshape.7526) | data formatting | bytes 1048576 | tf_op jit(solution)/shard_map/reshape | solution.py:192
  16.1 0.9 %copy_dynamic-update-slice_fusion = f32[4,32,32,32]{3,1,2,0:T(8,128)S(1)} fusion(f32[4,32,32,32]{3,1,2,0:T(8,128)S(1)} %copy.98, f32[3,32,32,32]{3,2,1,0:T(8,128)S(1)} %copy-done), kind=kLoop, calls=%fused_computation.18 | loop fusion | bytes 3145728 | tf_op jit(solution)/shard_map/scatter-add | solution.py:193
  17.2 0.7 collective-permute-start
  17.9 2.0 %collective-permute-start.1 = (f32[4,1,18,18]{3,1,2,0:T(1,128)S(1)}, f32[4,1,18,18]{3,1,2,0:T(1,128)S(1)}, u32[]{:S(2)}, u32[]{:S(2)}) collective-permute-start(f32[4,1,18,18]{3,1,2,0:T(1,128)S(1)} %get-tuple-element.32), channel_id=1, source_target_pairs={{8,0},{16,8},{24,16},{0,24},{9,1},{17,9},{25,17},{1,25},{10,2},{18... | collective-permute-start | bytes 15560 | tf_op jit(solution)/shard_map/ppermute | solution.py:28
  20.2 1.3 %collective-permute-done = f32[4,1,18,18]{3,1,2,0:T(1,128)S(1)} collective-permute-done((f32[4,1,18,18]{3,1,2,0:T(1,128)S(1)}, f32[4,1,18,18]{3,1,2,0:T(1,128)S(1)}, u32[]{:S(2)}, u32[]{:S(2)}) %collective-permute-start) | collective-permute-done | bytes 5216 | tf_op jit(solution)/shard_map/ppermute | solution.py:25
  21.8 2.2 %collective-permute-start.2 = (f32[4,20,1,18]{3,1,2,0:T(8,128)S(1)}, f32[4,20,1,18]{3,1,2,0:T(8,128)S(1)}, u32[]{:S(2)}, u32[]{:S(2)}) collective-permute-start(f32[4,20,1,18]{3,1,2,0:T(8,128)S(1)} %get-tuple-element.35), channel_id=1, source_target_pairs={{0,2},{2,4},{4,6},{6,0},{1,3},{3,5},{5,7},{7,1},{8,10},{10,12},{12... | collective-permute-start | bytes 17288 | tf_op jit(solution)/shard_map/ppermute | solution.py:25
  24.0 2.1 %collective-permute-start.3 = (f32[4,20,1,18]{3,1,2,0:T(8,128)S(1)}, f32[4,20,1,18]{3,1,2,0:T(8,128)S(1)}, u32[]{:S(2)}, u32[]{:S(2)}) collective-permute-start(f32[4,20,1,18]{3,1,2,0:T(8,128)S(1)} %get-tuple-element.36), channel_id=1, source_target_pairs={{2,0},{4,2},{6,4},{0,6},{3,1},{5,3},{7,5},{1,7},{10,8},{12,10},{14... | collective-permute-start | bytes 17288 | tf_op jit(solution)/shard_map/ppermute | solution.py:28
  26.1 2.1 %collective-permute-done.2 = f32[4,20,1,18]{3,1,2,0:T(8,128)S(1)} collective-permute-done((f32[4,20,1,18]{3,1,2,0:T(8,128)S(1)}, f32[4,20,1,18]{3,1,2,0:T(8,128)S(1)}, u32[]{:S(2)}, u32[]{:S(2)}) %collective-permute-start.2) | collective-permute-done | bytes 5792 | tf_op jit(solution)/shard_map/ppermute | solution.py:25
  28.2 1.4 %collective-permute-done.3 = f32[4,20,1,18]{3,1,2,0:T(8,128)S(1)} collective-permute-done((f32[4,20,1,18]{3,1,2,0:T(8,128)S(1)}, f32[4,20,1,18]{3,1,2,0:T(8,128)S(1)}, u32[]{:S(2)}, u32[]{:S(2)}) %collective-permute-start.3) | collective-permute-done | bytes 5792 | tf_op jit(solution)/shard_map/ppermute | solution.py:28
  30.0 0.6 copy.100
  30.6 1.3 %collective-permute-start.4 = (f32[4,20,20,1]{2,0,3,1:T(4,128)S(1)}, f32[4,20,20,1]{2,0,3,1:T(4,128)S(1)}, u32[]{:S(2)}, u32[]{:S(2)}) collective-permute-start(f32[4,20,20,1]{2,0,3,1:T(4,128)S(1)} %copy.100), channel_id=1, source_target_pairs={{0,1},{1,0},{2,3},{3,2},{4,5},{5,4},{6,7},{7,6},{8,9},{9,8},{10,11... | collective-permute-start | bytes 19208 | tf_op jit(solution)/shard_map/ppermute | solution.py:25
  32.0 0.6 copy.101
  32.5 0.8 collective-permute-start.5
  33.3 1.3 %collective-permute-done.4 = f32[4,20,20,1]{2,0,3,1:T(4,128)S(1)} collective-permute-done((f32[4,20,20,1]{2,0,3,1:T(4,128)S(1)}, f32[4,20,20,1]{2,0,3,1:T(4,128)S(1)}, u32[]{:S(2)}, u32[]{:S(2)}) %collective-permute-start.4) | collective-permute-done | bytes 6432 | tf_op jit(solution)/shard_map/ppermute | solution.py:25
  34.7 0.7 copy.102
  35.4 1.3 %collective-permute-done.5 = f32[4,20,20,1]{2,0,3,1:T(4,128)} collective-permute-done((f32[4,20,20,1]{2,0,3,1:T(4,128)S(1)}, f32[4,20,20,1]{2,0,3,1:T(4,128)}, u32[]{:S(2)}, u32[]{:S(2)}) %collective-permute-start.5) | collective-permute-done | bytes 6432 | tf_op jit(solution)/shard_map/ppermute | solution.py:28
  36.7 1.5 %copy.103 = f32[4,20,20,1]{3,1,2,0:T(8,128)S(1)} copy(f32[4,20,20,1]{2,0,3,1:T(4,128)} %collective-permute-done.5) | data formatting | bytes 12800 | tf_op jit(solution)/shard_map/ppermute | solution.py:28
  38.2 0.7 pad_maximum_fusion.1
  39.0 0.6 maximum_add_fusion.1
  39.5 0.6 maximum_add_fusion
  41.8 1.7 %collective-permute-start.7 = (f32[3,1,16,16]{3,1,2,0:T(1,128)S(1)}, f32[3,1,16,16]{3,1,2,0:T(1,128)S(1)}, u32[]{:S(2)}, u32[]{:S(2)}) collective-permute-start(f32[3,1,16,16]{3,1,2,0:T(1,128)S(1)} %get-tuple-element.46), channel_id=1, source_target_pairs={{8,0},{16,8},{24,16},{0,24},{9,1},{17,9},{25,17},{1,25},{10,2},{18... | collective-permute-start | bytes 9224 | tf_op jit(solution)/shard_map/ppermute | solution.py:28
  43.5 1.5 %collective-permute-done.6 = f32[3,1,16,16]{3,1,2,0:T(1,128)S(1)} collective-permute-done((f32[3,1,16,16]{3,1,2,0:T(1,128)S(1)}, f32[3,1,16,16]{3,1,2,0:T(1,128)S(1)}, u32[]{:S(2)}, u32[]{:S(2)}) %collective-permute-start.6) | collective-permute-done | bytes 3104 | tf_op jit(solution)/shard_map/ppermute | solution.py:25
  45.1 1.3 %collective-permute-start.8 = (f32[3,18,1,16]{3,1,2,0:T(8,128)S(1)}, f32[3,18,1,16]{3,1,2,0:T(8,128)S(1)}, u32[]{:S(2)}, u32[]{:S(2)}) collective-permute-start(f32[3,18,1,16]{3,1,2,0:T(8,128)S(1)} %get-tuple-element.43), channel_id=1, source_target_pairs={{0,2},{2,4},{4,6},{6,0},{1,3},{3,5},{5,7},{7,1},{8,10},{10,12},{12... | collective-permute-start | bytes 10376 | tf_op jit(solution)/shard_map/ppermute | solution.py:25
  46.4 2.5 %collective-permute-start.9 = (f32[3,18,1,16]{3,1,2,0:T(8,128)S(1)}, f32[3,18,1,16]{3,1,2,0:T(8,128)S(1)}, u32[]{:S(2)}, u32[]{:S(2)}) collective-permute-start(f32[3,18,1,16]{3,1,2,0:T(8,128)S(1)} %get-tuple-element.44), channel_id=1, source_target_pairs={{2,0},{4,2},{6,4},{0,6},{3,1},{5,3},{7,5},{1,7},{10,8},{12,10},{14... | collective-permute-start | bytes 10376 | tf_op jit(solution)/shard_map/ppermute | solution.py:28
  49.0 2.1 %collective-permute-done.8 = f32[3,18,1,16]{3,1,2,0:T(8,128)S(1)} collective-permute-done((f32[3,18,1,16]{3,1,2,0:T(8,128)S(1)}, f32[3,18,1,16]{3,1,2,0:T(8,128)S(1)}, u32[]{:S(2)}, u32[]{:S(2)}) %collective-permute-start.8) | collective-permute-done | bytes 3488 | tf_op jit(solution)/shard_map/ppermute | solution.py:25
  52.2 0.5 collective-permute-start.10
  53.2 1.6 %collective-permute-start.11 = (f32[3,18,18,1]{2,3,1,0:T(1,128)S(1)}, f32[3,18,18,1]{2,3,1,0:T(1,128)S(1)}, u32[]{:S(2)}, u32[]{:S(2)}) collective-permute-start(f32[3,18,18,1]{2,3,1,0:T(1,128)S(1)} %copy.105), channel_id=1, source_target_pairs={{1,0},{0,1},{3,2},{2,3},{5,4},{4,5},{7,6},{6,7},{9,8},{8,9},{11,10... | collective-permute-start | bytes 11672 | tf_op jit(solution)/shard_map/ppermute | solution.py:28
  54.9 1.3 %collective-permute-done.10 = f32[3,18,18,1]{2,3,1,0:T(1,128)S(1)} collective-permute-done((f32[3,18,18,1]{2,3,1,0:T(1,128)S(1)}, f32[3,18,18,1]{2,3,1,0:T(1,128)S(1)}, u32[]{:S(2)}, u32[]{:S(2)}) %collective-permute-start.10) | collective-permute-done | bytes 3920 | tf_op jit(solution)/shard_map/ppermute | solution.py:25
  56.2 0.5 copy.106
  57.1 0.5 copy.107
  57.6 3.9 %select_maximum_fusion = f32[3,32,32,32]{3,1,2,0:T(8,128)S(1)} fusion(f32[3,18,18,1]{3,1,2,0:T(8,128)S(1)} %copy.107, f32[3,18,18,1]{3,1,2,0:T(8,128)S(1)} %copy.106, f32[3,18,1,16]{3,1,2,0:T(8,128)S(1)} %collective-permute-done.9, f32[3,18,1,16]{3,1,2,0:T(8,128)S(1)} %collective-permute-done.8, f32[3,1,16,16]{3,1,2,0:T(1,128)S(1)} %collective-permute-done.7, ...), kind=kLoop, calls=%fused_computation.12 | loop fusion | flops 3735552 | bytes 463200 | tf_op jit(solution)/shard_map/concatenate | solution.py:29
  61.5 2.0 %fusion.30 = f32[3,512]{1,0:T(4,128)S(1)} fusion(f32[3,32,32,32]{3,1,2,0:T(8,128)S(1)} %select_maximum_fusion, f32[32,512]{1,0:T(8,128)S(1)} %get-tuple-element.187, f32[32,512]{1,0:T(8,128)S(1)} %get-tuple-element.186, f32[32,512]{1,0:T(8,128)S(1)} %get-tuple-element.189), kind=kOutput, calls=%fused_computation.33 | convolution fusion | flops 604600832 | bytes 595968 | tf_op jit(solution)/shard_map/dot_general | solution.py:130
  63.5 2.0 %multiply_reduce_fusion = (f32[3,512]{1,0:T(4,128)S(1)}, f32[3,512]{1,0:T(4,128)S(1)}) fusion(f32[32,512]{1,0:T(8,128)S(1)} %get-tuple-element.190, f32[32,512]{1,0:T(8,128)S(1)} %get-tuple-element.189, f32[3,32,32,32]{3,1,2,0:T(8,128)S(1)} %select_maximum_fusion, f32[32,512]{1,0:T(8,128)S(1)} %get-tuple-element.186, f32[32,512]{1,0:T(8,128)S(1)} %get-tuple-element.188), kind=kOutput, calls=%fused_computation.52 | convolution fusion | flops 604697600 | bytes 667648 | tf_op jit(solution)/shard_map/dot_general | solution.py:130
  65.5 2.0 %fusion.27 = f32[3,512]{1,0:T(4,128)S(1)} fusion(f32[3,32,32,32]{3,1,2,0:T(8,128)S(1)} %select_maximum_fusion, f32[32,512]{1,0:T(8,128)S(1)} %get-tuple-element.185, f32[32,512]{1,0:T(8,128)S(1)} %get-tuple-element.188, f32[32,512]{1,0:T(8,128)S(1)} %get-tuple-element.189), kind=kOutput, calls=%fused_computation.32 | convolution fusion | flops 604600832 | bytes 595968 | tf_op jit(solution)/shard_map/dot_general | solution.py:130
  68.5 1.7 %collective-permute-start.13 = (f32[1,26,8]{1,2,0:T(8,128)S(1)}, f32[1,26,8]{1,2,0:T(8,128)S(1)}, u32[]{:S(2)}, u32[]{:S(2)}) collective-permute-start(f32[1,26,8]{1,2,0:T(8,128)S(1)} %get-tuple-element.178), channel_id=1, source_target_pairs={{8,0},{16,8},{24,16},{0,24},{9,1},{17,9},{25,17},{1,25},{10,2},{18... | collective-permute-start | bytes 2504 | tf_op jit(solution)/shard_map/ppermute | solution.py:28
  70.2 0.5 collective-permute-start.14
  70.7 3.3 %collective-permute-start.15 = (f32[1,26,8]{1,2,0:T(8,128)S(1)}, f32[1,26,8]{1,2,0:T(8,128)S(1)}, u32[]{:S(2)}, u32[]{:S(2)}) collective-permute-start(f32[1,26,8]{1,2,0:T(8,128)S(1)} %get-tuple-element.176), channel_id=1, source_target_pairs={{2,0},{4,2},{6,4},{0,6},{3,1},{5,3},{7,5},{1,7},{10,8},{12,10},{14... | collective-permute-start | bytes 2504 | tf_op jit(solution)/shard_map/ppermute | solution.py:28
  74.0 1.6 %collective-permute-start.16 = (f32[1,26,8]{1,2,0:T(8,128)S(1)}, f32[1,26,8]{1,2,0:T(8,128)S(1)}, u32[]{:S(2)}, u32[]{:S(2)}) collective-permute-start(f32[1,26,8]{1,2,0:T(8,128)S(1)} %get-tuple-element.175), channel_id=1, source_target_pairs={{0,1},{1,0},{2,3},{3,2},{4,5},{5,4},{6,7},{7,6},{8,9},{9,8},{10,11... | collective-permute-start | bytes 2504 | tf_op jit(solution)/shard_map/ppermute | solution.py:25
  76.1 1.5 %collective-permute-done.16 = f32[1,26,8]{1,2,0:T(8,128)S(1)} collective-permute-done((f32[1,26,8]{1,2,0:T(8,128)S(1)}, f32[1,26,8]{1,2,0:T(8,128)S(1)}, u32[]{:S(2)}, u32[]{:S(2)}) %collective-permute-start.16) | collective-permute-done | bytes 864 | tf_op jit(solution)/shard_map/ppermute | solution.py:25
  77.7 1.6 %collective-permute-done.17 = f32[1,26,8]{1,2,0:T(8,128)S(1)} collective-permute-done((f32[1,26,8]{1,2,0:T(8,128)S(1)}, f32[1,26,8]{1,2,0:T(8,128)S(1)}, u32[]{:S(2)}, u32[]{:S(2)}) %collective-permute-start.17) | collective-permute-done | bytes 864 | tf_op jit(solution)/shard_map/ppermute | solution.py:28
  79.2 0.9 %convolution_add_fusion.2 = f32[26,512]{1,0:T(8,128)} fusion(f32[26,512]{1,0:T(8,128)S(1)} %concatenate.51, s32[48]{0:T(128)S(1)} %eq.315, f32[512]{0:T(512)S(1)} %broadcast_subtract_fusion, f32[512]{0:T(512)S(1)} %fusion.73, f32[26,6,8]{0,2,1:T(8,128)S(1)} %constant_dynamic-update-slice_fusion), kind=kOutput, calls=%fused_computation.34 | convolution fusion | flops 7732224 | bytes 115776 | tf_op jit(solution)/shard_map/dot_general | solution.py:130
  (209 shorter events, 8.9 us)
Async XLA Ops:
  0.0 3.6 %copy-start.2 = (f32[26,512]{1,0:T(8,128)S(1)}, f32[26,512]{1,0:T(8,128)}, u32[]{:S(2)}) copy-start(f32[26,512]{1,0:T(8,128)} %param.9) | copy-start | bytes 159748
  1.2 3.5 %copy-start.4 = (s32[512]{0:T(512)S(1)}, s32[512]{0:T(512)}, u32[]{:S(2)}) copy-start(s32[512]{0:T(512)} %param.10) | copy-start | bytes 6148
  1.2 3.5 %copy-start.5 = (s32[512]{0:T(512)S(1)}, s32[512]{0:T(512)}, u32[]{:S(2)}) copy-start(s32[512]{0:T(512)} %param.11) | copy-start | bytes 6148
  7.9 2.2 %copy-start.1 = (f32[224,1024]{1,0:T(8,128)}, f32[224,1024]{1,0:T(8,128)S(1)}, u32[]{:S(2)}) copy-start(f32[224,1024]{1,0:T(8,128)S(1)} %fusion.33) | copy-start | bytes 2752516
  12.3 1.7 %slice-start = ((f32[224,1024]{1,0:T(8,128)}), f32[128,1024]{1,0:T(8,128)S(1)}, s32[]{:S(2)}) async-start(f32[224,1024]{1,0:T(8,128)} %copy-done.1), calls=%async_computation | async-start | bytes 1048576 | tf_op jit(solution)/shard_map/slice | solution.py:190
  14.7 1.4 %copy-start = (f32[3,32,32,32]{3,2,1,0:T(8,128)S(1)}, f32[3,32,32,32]{3,2,1,0:T(8,128)}, u32[]{:S(2)}) copy-start(f32[3,32,32,32]{3,2,1,0:T(8,128)} %add.3113) | copy-start | bytes 1179652
  17.2 4.3 %collective-permute-start = (f32[4,1,18,18]{3,1,2,0:T(1,128)S(1)}, f32[4,1,18,18]{3,1,2,0:T(1,128)S(1)}, u32[]{:S(2)}, u32[]{:S(2)}) collective-permute-start(f32[4,1,18,18]{3,1,2,0:T(1,128)S(1)} %get-tuple-element.31), channel_id=1, source_target_pairs={{0,8},{8,16},{16,24},{24,0},{1,9},{9,17},{17,25},{25,1},{2,10},{10... | collective-permute-start | bytes 15560 | tf_op jit(solution)/shard_map/ppermute | solution.py:25
  17.9 3.8 %collective-permute-start.1 = (f32[4,1,18,18]{3,1,2,0:T(1,128)S(1)}, f32[4,1,18,18]{3,1,2,0:T(1,128)S(1)}, u32[]{:S(2)}, u32[]{:S(2)}) collective-permute-start(f32[4,1,18,18]{3,1,2,0:T(1,128)S(1)} %get-tuple-element.32), channel_id=1, source_target_pairs={{8,0},{16,8},{24,16},{0,24},{9,1},{17,9},{25,17},{1,25},{10,2},{18... | collective-permute-start | bytes 15560 | tf_op jit(solution)/shard_map/ppermute | solution.py:28
  21.8 6.4 %collective-permute-start.2 = (f32[4,20,1,18]{3,1,2,0:T(8,128)S(1)}, f32[4,20,1,18]{3,1,2,0:T(8,128)S(1)}, u32[]{:S(2)}, u32[]{:S(2)}) collective-permute-start(f32[4,20,1,18]{3,1,2,0:T(8,128)S(1)} %get-tuple-element.35), channel_id=1, source_target_pairs={{0,2},{2,4},{4,6},{6,0},{1,3},{3,5},{5,7},{7,1},{8,10},{10,12},{12... | collective-permute-start | bytes 17288 | tf_op jit(solution)/shard_map/ppermute | solution.py:25
  24.0 5.6 %collective-permute-start.3 = (f32[4,20,1,18]{3,1,2,0:T(8,128)S(1)}, f32[4,20,1,18]{3,1,2,0:T(8,128)S(1)}, u32[]{:S(2)}, u32[]{:S(2)}) collective-permute-start(f32[4,20,1,18]{3,1,2,0:T(8,128)S(1)} %get-tuple-element.36), channel_id=1, source_target_pairs={{2,0},{4,2},{6,4},{0,6},{3,1},{5,3},{7,5},{1,7},{10,8},{12,10},{14... | collective-permute-start | bytes 17288 | tf_op jit(solution)/shard_map/ppermute | solution.py:28
  30.6 4.0 %collective-permute-start.4 = (f32[4,20,20,1]{2,0,3,1:T(4,128)S(1)}, f32[4,20,20,1]{2,0,3,1:T(4,128)S(1)}, u32[]{:S(2)}, u32[]{:S(2)}) collective-permute-start(f32[4,20,20,1]{2,0,3,1:T(4,128)S(1)} %copy.100), channel_id=1, source_target_pairs={{0,1},{1,0},{2,3},{3,2},{4,5},{5,4},{6,7},{7,6},{8,9},{9,8},{10,11... | collective-permute-start | bytes 19208 | tf_op jit(solution)/shard_map/ppermute | solution.py:25
  32.5 4.1 %collective-permute-start.5 = (f32[4,20,20,1]{2,0,3,1:T(4,128)S(1)}, f32[4,20,20,1]{2,0,3,1:T(4,128)}, u32[]{:S(2)}, u32[]{:S(2)}) collective-permute-start(f32[4,20,20,1]{2,0,3,1:T(4,128)S(1)} %copy.101), channel_id=1, source_target_pairs={{1,0},{0,1},{3,2},{2,3},{5,4},{4,5},{7,6},{6,7},{9,8},{8,9},{11,10... | collective-permute-start | bytes 19208 | tf_op jit(solution)/shard_map/ppermute | solution.py:28
  41.2 7.7 %copy-start.3 = (s32[6,8]{1,0:T(8,128)S(1)}, s32[6,8]{1,0:T(8,128)}, u32[]{:S(2)}) copy-start(s32[6,8]{1,0:T(8,128)} %param.13) | copy-start | bytes 580
  41.7 3.3 %collective-permute-start.6 = (f32[3,1,16,16]{3,1,2,0:T(1,128)S(1)}, f32[3,1,16,16]{3,1,2,0:T(1,128)S(1)}, u32[]{:S(2)}, u32[]{:S(2)}) collective-permute-start(f32[3,1,16,16]{3,1,2,0:T(1,128)S(1)} %get-tuple-element.45), channel_id=1, source_target_pairs={{0,8},{8,16},{16,24},{24,0},{1,9},{9,17},{17,25},{25,1},{2,10},{10... | collective-permute-start | bytes 9224 | tf_op jit(solution)/shard_map/ppermute | solution.py:25
  41.8 3.3 %collective-permute-start.7 = (f32[3,1,16,16]{3,1,2,0:T(1,128)S(1)}, f32[3,1,16,16]{3,1,2,0:T(1,128)S(1)}, u32[]{:S(2)}, u32[]{:S(2)}) collective-permute-start(f32[3,1,16,16]{3,1,2,0:T(1,128)S(1)} %get-tuple-element.46), channel_id=1, source_target_pairs={{8,0},{16,8},{24,16},{0,24},{9,1},{17,9},{25,17},{1,25},{10,2},{18... | collective-permute-start | bytes 9224 | tf_op jit(solution)/shard_map/ppermute | solution.py:28
  45.1 6.1 %collective-permute-start.8 = (f32[3,18,1,16]{3,1,2,0:T(8,128)S(1)}, f32[3,18,1,16]{3,1,2,0:T(8,128)S(1)}, u32[]{:S(2)}, u32[]{:S(2)}) collective-permute-start(f32[3,18,1,16]{3,1,2,0:T(8,128)S(1)} %get-tuple-element.43), channel_id=1, source_target_pairs={{0,2},{2,4},{4,6},{6,0},{1,3},{3,5},{5,7},{7,1},{8,10},{10,12},{12... | collective-permute-start | bytes 10376 | tf_op jit(solution)/shard_map/ppermute | solution.py:25
  46.4 5.1 %collective-permute-start.9 = (f32[3,18,1,16]{3,1,2,0:T(8,128)S(1)}, f32[3,18,1,16]{3,1,2,0:T(8,128)S(1)}, u32[]{:S(2)}, u32[]{:S(2)}) collective-permute-start(f32[3,18,1,16]{3,1,2,0:T(8,128)S(1)} %get-tuple-element.44), channel_id=1, source_target_pairs={{2,0},{4,2},{6,4},{0,6},{3,1},{5,3},{7,5},{1,7},{10,8},{12,10},{14... | collective-permute-start | bytes 10376 | tf_op jit(solution)/shard_map/ppermute | solution.py:28
  52.2 4.0 %collective-permute-start.10 = (f32[3,18,18,1]{2,3,1,0:T(1,128)S(1)}, f32[3,18,18,1]{2,3,1,0:T(1,128)S(1)}, u32[]{:S(2)}, u32[]{:S(2)}) collective-permute-start(f32[3,18,18,1]{2,3,1,0:T(1,128)S(1)} %copy.104), channel_id=1, source_target_pairs={{0,1},{1,0},{2,3},{3,2},{4,5},{5,4},{6,7},{7,6},{8,9},{9,8},{10,11... | collective-permute-start | bytes 11672 | tf_op jit(solution)/shard_map/ppermute | solution.py:25
  53.2 3.9 %collective-permute-start.11 = (f32[3,18,18,1]{2,3,1,0:T(1,128)S(1)}, f32[3,18,18,1]{2,3,1,0:T(1,128)S(1)}, u32[]{:S(2)}, u32[]{:S(2)}) collective-permute-start(f32[3,18,18,1]{2,3,1,0:T(1,128)S(1)} %copy.105), channel_id=1, source_target_pairs={{1,0},{0,1},{3,2},{2,3},{5,4},{4,5},{7,6},{6,7},{9,8},{8,9},{11,10... | collective-permute-start | bytes 11672 | tf_op jit(solution)/shard_map/ppermute | solution.py:28
  65.5 2.3 %slice-start.1 = ((f32[26,512]{1,0:T(8,128)}), f32[2,512]{1,0:T(2,128)S(1)}, s32[]{:S(2)}) async-start(f32[26,512]{1,0:T(8,128)} %param.9), calls=%async_computation.1 | async-start | bytes 8192 | tf_op jit(solution)/shard_map/slice | solution.py:246
  68.4 7.2 %collective-permute-start.12 = (f32[1,26,8]{1,2,0:T(8,128)S(1)}, f32[1,26,8]{1,2,0:T(8,128)S(1)}, u32[]{:S(2)}, u32[]{:S(2)}) collective-permute-start(f32[1,26,8]{1,2,0:T(8,128)S(1)} %get-tuple-element.179), channel_id=1, source_target_pairs={{0,8},{8,16},{16,24},{24,0},{1,9},{9,17},{17,25},{25,1},{2,10},{10... | collective-permute-start | bytes 2504 | tf_op jit(solution)/shard_map/ppermute | solution.py:25
  68.5 7.6 %collective-permute-start.13 = (f32[1,26,8]{1,2,0:T(8,128)S(1)}, f32[1,26,8]{1,2,0:T(8,128)S(1)}, u32[]{:S(2)}, u32[]{:S(2)}) collective-permute-start(f32[1,26,8]{1,2,0:T(8,128)S(1)} %get-tuple-element.178), channel_id=1, source_target_pairs={{8,0},{16,8},{24,16},{0,24},{9,1},{17,9},{25,17},{1,25},{10,2},{18... | collective-permute-start | bytes 2504 | tf_op jit(solution)/shard_map/ppermute | solution.py:28
  70.2 5.9 %collective-permute-start.14 = (f32[1,26,8]{1,2,0:T(8,128)S(1)}, f32[1,26,8]{1,2,0:T(8,128)S(1)}, u32[]{:S(2)}, u32[]{:S(2)}) collective-permute-start(f32[1,26,8]{1,2,0:T(8,128)S(1)} %get-tuple-element.177), channel_id=1, source_target_pairs={{0,2},{2,4},{4,6},{6,0},{1,3},{3,5},{5,7},{7,1},{8,10},{10,12},{12... | collective-permute-start | bytes 2504 | tf_op jit(solution)/shard_map/ppermute | solution.py:25
  70.7 5.4 %collective-permute-start.15 = (f32[1,26,8]{1,2,0:T(8,128)S(1)}, f32[1,26,8]{1,2,0:T(8,128)S(1)}, u32[]{:S(2)}, u32[]{:S(2)}) collective-permute-start(f32[1,26,8]{1,2,0:T(8,128)S(1)} %get-tuple-element.176), channel_id=1, source_target_pairs={{2,0},{4,2},{6,4},{0,6},{3,1},{5,3},{7,5},{1,7},{10,8},{12,10},{14... | collective-permute-start | bytes 2504 | tf_op jit(solution)/shard_map/ppermute | solution.py:28
  74.0 3.6 %collective-permute-start.16 = (f32[1,26,8]{1,2,0:T(8,128)S(1)}, f32[1,26,8]{1,2,0:T(8,128)S(1)}, u32[]{:S(2)}, u32[]{:S(2)}) collective-permute-start(f32[1,26,8]{1,2,0:T(8,128)S(1)} %get-tuple-element.175), channel_id=1, source_target_pairs={{0,1},{1,0},{2,3},{3,2},{4,5},{5,4},{6,7},{7,6},{8,9},{9,8},{10,11... | collective-permute-start | bytes 2504 | tf_op jit(solution)/shard_map/ppermute | solution.py:25
  75.6 3.6 %collective-permute-start.17 = (f32[1,26,8]{1,2,0:T(8,128)S(1)}, f32[1,26,8]{1,2,0:T(8,128)S(1)}, u32[]{:S(2)}, u32[]{:S(2)}) collective-permute-start(f32[1,26,8]{1,2,0:T(8,128)S(1)} %get-tuple-element.174), channel_id=1, source_target_pairs={{1,0},{0,1},{3,2},{2,3},{5,4},{4,5},{7,6},{6,7},{9,8},{8,9},{11,10... | collective-permute-start | bytes 2504 | tf_op jit(solution)/shard_map/ppermute | solution.py:28
where the time goes:
time: 80.4 us; the launch traced here: 80.1 us
  starting transfers between devices  24.6 us (31%)
  waiting for transfers between devices  16.3 us (20%)
  matrix products  13.5 us (17%)
  local copies, waits for them, and re-layouts  13.1 us (16%)
  other arithmetic  10.5 us (13%)
  between operations  2.04 us (3%)
    ppermute x9, starting transfers between devices, extended_2(): lax.ppermute(lax.slice_in_dim(block, 0, width, axis=dim), axis, backward)  16.4 us
    ppermute x9, waiting for transfers between devices, extended_2(): lax.ppermute(lax.slice_in_dim(block, block.shape[dim] - width, None, axis...  11.2 us
    ppermute x9, starting transfers between devices, extended_2(): lax.ppermute(lax.slice_in_dim(block, block.shape[dim] - width, None, axis...  8.2 us
    dot_general x4, matrix products, contract_inner(): lax.dot_general(left_side, right_side, (((1,), (0,)), ((), ())), precisio...  6.85 us
    dot_general x4, matrix products, contract_last(): lax.dot_general(left_side, right_side, (((1,), (1,)), ((), ())), precisio...  6.67 us
    ppermute x9, waiting for transfers between devices, extended_2(): lax.ppermute(lax.slice_in_dim(block, 0, width, axis=dim), axis, backward)  5.07 us
    concatenate x4, other arithmetic, extended_2(): block = jnp.concatenate([low, block, high], axis=dim)  4.95 us
    ppermute x2, local copies, waits for them, and re-layouts, extended_2(): lax.ppermute(lax.slice_in_dim(block, 0, width, axis=dim), axis, backward)  2.01 us
  transfers between devices with their start and end apart: 18, of which 13 were waited for; matrix products, arithmetic and copies ran while one was open for 3% of the time, Pallas kernels for 0%

commit v1 on v0

v1 whole, which is shorter than its diff:
```python
import functools

import jax
import jax.numpy as jnp
from jax import lax
from jax.experimental import pallas as pl
from jax.experimental.pallas import tpu as pltpu
from jax.sharding import PartitionSpec as P

BLK = 2
AXES = ("gx", "gy", "gz")
SPAN = 8 * BLK + 2
STRIDE = 24
ROWS = 4 * SPAN
LANES = 512
USED = STRIDE * SPAN
EDGE = 2 * STRIDE
FACES = 6

time_step = 0.05
stress_gain = 0.2
shear_zero = 5.0
bulk_zero = 5.0
harden_rate = 10.0
mass_floor = 0.1
gravity = 9.8

f32 = jnp.float32
bf16 = jnp.bfloat16
MESH = pl.DeviceIdType.MESH


def iota(shape, dim):
    return lax.broadcasted_iota(jnp.int32, shape, dim)


def split(value):
    high = value.astype(bf16)
    return high, (value - high.astype(f32)).astype(bf16)


def stacked(value):
    high = value.astype(bf16).astype(f32)
    return jnp.concatenate([high, value - high], axis=0).astype(bf16)


def dot_nt(left, right):
    return lax.dot_general(left, right, (((1,), (1,)), ((), ())), preferred_element_type=f32)


def dot_nn(left, right):
    return lax.dot_general(left, right, (((1,), (0,)), ((), ())), preferred_element_type=f32)


def contract(dot, left, right_high, right_low):
    rows = left.shape[0]
    both = dot(stacked(left), right_high)
    return both[:rows] + both[rows:] + dot(left.astype(bf16), right_low)


def spline(place, anchor, fraction):
    apart = (place - anchor) - fraction
    size = jnp.abs(apart)
    outer = jnp.maximum(1.5 - size, 0.0)
    inner = jnp.maximum(0.5 - size, 0.0)
    weight = 0.5 * outer * outer - 1.5 * inner * inner
    return weight, weight * apart


def axis_tables(anchor, fraction):
    count = fraction.shape[1]
    line = iota((STRIDE, count), 0).astype(f32)
    line_x = jnp.right_shift(iota((ROWS, count), 0), 2).astype(f32)
    return (
        spline(line_x, anchor[0:1], fraction[0:1]),
        spline(line, anchor[1:2], fraction[1:2]),
        spline(line, anchor[2:3], fraction[2:3]),
    )


def store_pair(high_ref, low_ref, row, column, outer_line, inner_line, picks):
    count = inner_line.shape[1]
    pair = jnp.concatenate([outer_line[p : p + 1] * inner_line for p in picks], axis=0)
    high, low = split(pair)
    high_ref[row : row + EDGE, column : column + count] = high
    low_ref[row : row + EDGE, column : column + count] = low


def fill_tables(high_ref, low_ref, tables):
    _, (weight_y, shift_y), (weight_z, shift_z) = tables
    count = weight_y.shape[1]
    for part, (outer, inner) in enumerate(
        ((weight_y, weight_z), (shift_y, weight_z), (weight_y, shift_z))
    ):
        for pair in range(SPAN // 2):
            store_pair(
                high_ref, low_ref, EDGE * pair, part * count, outer, inner, (2 * pair, 2 * pair + 1)
            )
    for ref in (high_ref, low_ref):
        ref[USED:LANES, :] = jnp.zeros((LANES - USED, 3 * count), bf16)


def fill_face(high_ref, low_ref, tables):
    _, (weight_y, shift_y), (weight_z, shift_z) = tables
    count = weight_y.shape[1]
    for part, (outer, inner) in enumerate(
        ((weight_z, weight_y), (weight_z, shift_y), (shift_z, weight_y))
    ):
        store_pair(high_ref, low_ref, 0, part * count, outer, inner, (0, 1))
        store_pair(high_ref, low_ref, EDGE, part * count, outer, inner, (SPAN - 2, SPAN - 1))
    for ref in (high_ref, low_ref):
        ref[2 * EDGE : 128, :] = jnp.zeros((128 - 2 * EDGE, 3 * count), bf16)


def product(left, right):
    return [
        [
            left[i][0] * right[0][j] + left[i][1] * right[1][j] + left[i][2] * right[2][j]
            for j in range(3)
        ]
        for i in range(3)
    ]


def transposed(matrix):
    return [[matrix[j][i] for j in range(3)] for i in range(3)]


def pack(row):
    count = row.shape[1]
    return jnp.concatenate([row[:, s : s + 128] for s in range(0, count, 128)], axis=0)


def unpack(block):
    return jnp.concatenate([block[s : s + 1] for s in range(block.shape[0])], axis=1)


def stress(deform, plastic):
    rotation = deform
    for _ in range(5):
        inner = product(transposed(rotation), rotation)
        inner = [[(3.0 - inner[i][j]) if i == j else -inner[i][j] for j in range(3)] for i in range(3)]
        rotation = product(rotation, inner)
        rotation = [[0.5 * entry for entry in line] for line in rotation]
    f = deform
    volume = (
        f[0][0] * (f[1][1] * f[2][2] - f[1][2] * f[2][1])
        - f[0][1] * (f[1][0] * f[2][2] - f[1][2] * f[2][0])
        + f[0][2] * (f[1][0] * f[2][1] - f[1][1] * f[2][0])
    )
    harden = jnp.exp(harden_rate * (1.0 - plastic))
    shear = 2.0 * shear_zero * harden
    bulk = bulk_zero * harden * (volume - 1.0) * volume
    apart = [[f[i][j] - rotation[i][j] for j in range(3)] for i in range(3)]
    tau = product(apart, transposed(f))
    return [
        [shear * tau[i][j] + bulk if i == j else shear * tau[i][j] for j in range(3)]
        for i in range(3)
    ]


def read_back(out_ref, record, anchor, living, tables, high_ref, low_ref, velocity):
    count = record.shape[1]
    (weight_x, shift_x), _, _ = tables
    reads = contract(dot_nn, velocity, high_ref[...], low_ref[...])

    def fold(value):
        total = value[0:8]
        for row in range(8, ROWS, 8):
            total = total + value[row : row + 8]
        return total[0:4] + total[4:8]

    first = reads[:, 0:count]
    speed = fold(weight_x * first) * living
    along = [
        4.0 * living * fold(shift_x * first),
        4.0 * living * fold(weight_x * reads[:, count : 2 * count]),
        4.0 * living * fold(weight_x * reads[:, 2 * count : 3 * count]),
    ]
    out_ref[0:3, :] = speed[1:4]
    deform = [record[12 + 3 * k : 15 + 3 * k] for k in range(3)]
    for i in range(3):
        push = jnp.zeros((3, count), f32)
        for j in range(3):
            entry = along[j][1 + i : 2 + i]
            out_ref[3 + 3 * i + j : 4 + 3 * i + j, :] = entry
            push = push + entry * deform[j]
        out_ref[12 + 3 * i : 15 + 3 * i, :] = deform[i] * living + time_step * push
    out_ref[21:24, :] = record[21:24] * living + time_step * speed[1:4]
    out_ref[24:26, :] = record[24:26] * living
    out_ref[26:32, :] = jnp.zeros((6, count), f32)


def kernel(
    sizes,
    live_ref,
    record_ref,
    block_ref,
    offset_ref,
    plan_ref,
    out_ref,
    high_ref,
    low_ref,
    face_high,
    face_low,
    some_high,
    some_low,
    grid_ref,
    z_send,
    z_recv,
    x_recv,
    y_recv,
    c_recv,
    leave_ref,
    come_ref,
    new_ref,
    z_sems,
    xy_sems,
    m_sems,
):
    me = [lax.axis_index(name) for name in AXES]

    def at(*step):
        return tuple(
            lax.rem(me[a] + step[a] + sizes[a], sizes[a]) if step[a] else me[a] for a in range(3)
        )

    pair_z = sizes[2] == 2
    z_steps = ((0, 0, 1),) if pair_z else ((0, 0, 1), (0, 0, -1))
    xy_steps = tuple((i, j, 0) for i in (1, 0, -1) for j in (1, 0, -1) if i or j)
    barrier = pltpu.get_barrier_semaphore()
    for step in z_steps + xy_steps:
        pl.semaphore_signal(barrier, inc=1, device_id=at(*step), device_id_type=MESH)

    count = record_ref.shape[1]
    record = record_ref[...]
    fraction = record[21:24]
    blocks = block_ref[...]
    offsets = offset_ref[...]
    anchor = (
        jnp.concatenate(
            [
                8 * jnp.right_shift(blocks, 2) + jnp.right_shift(offsets, 6),
                8 * (jnp.right_shift(blocks, 1) & 1) + (jnp.right_shift(offsets, 3) & 7),
                8 * (blocks & 1) + (offsets & 7),
            ],
            axis=0,
        )
        + 1
    ).astype(f32)
    living = jnp.where(iota((1, count), 1) < live_ref[0], 1.0, 0.0).astype(f32)

    tables = axis_tables(anchor, fraction)
    fill_face(face_high, face_low, tables)

    plastic = pack(record[25:26])
    deform = [[pack(record[12 + 3 * i + j : 13 + 3 * i + j]) for j in range(3)] for i in range(3)]
    tau = stress(deform, plastic)
    mass = record[24:25]
    held = mass * living
    coupling = [
        [
            (mass * record[3 + 3 * i + j : 4 + 3 * i + j] - stress_gain * unpack(tau[i][j])) * living
            for j in range(3)
        ]
        for i in range(3)
    ]
    none = jnp.zeros((1, count), f32)
    base = jnp.concatenate([held, held * record[0:3]] * 2, axis=0)
    pushes = [
        jnp.concatenate([none, coupling[0][j], coupling[1][j], coupling[2][j]] * 2, axis=0)
        for j in range(3)
    ]
    weight_x, shift_x = tables[0]
    tiles = range(0, ROWS, 8)
    first = [base * weight_x[r : r + 8] + pushes[0] * shift_x[r : r + 8] for r in tiles]
    second = [pushes[1] * weight_x[r : r + 8] for r in tiles]
    third = [pushes[2] * weight_x[r : r + 8] for r in tiles]
    left = jnp.concatenate([jnp.concatenate(part, axis=0) for part in (first, second, third)], axis=1)

    z_send[...] = contract(dot_nt, left, face_high[...], face_low[...])
    pl.semaphore_wait(barrier, len(z_steps) + len(xy_steps))

    def send(source, target, sems, slot, step):
        copy = pltpu.make_async_remote_copy(
            src_ref=source,
            dst_ref=target,
            send_sem=sems.at[0, slot],
            recv_sem=sems.at[1, slot],
            device_id=at(*step),
            device_id_type=MESH,
        )
        copy.start()
        return copy

    z_copies = [
        send(z_send, z_recv.at[slot], z_sems, slot, step) for slot, step in enumerate(z_steps)
    ]

    fill_tables(high_ref, low_ref, tables)
    partial = contract(dot_nt, left, high_ref[...], low_ref[...])

    lane = iota((128, LANES), 1)
    row = iota((128, LANES), 0)
    lane_y = jnp.right_shift(lane * 2731, 16)
    row_k = jnp.right_shift(row * 2731, 16)
    goal_z = jnp.where(row_k < 2, row_k + (SPAN - 2), row_k - 2)
    spread = jnp.where(
        (row - STRIDE * row_k == lane_y)
        & (lane - STRIDE * lane_y == goal_z)
        & (row_k < 4)
        & (lane_y < SPAN),
        1.0,
        0.0,
    ).astype(bf16)
    for copy in z_copies:
        copy.wait()
    if pair_z:
        shared = z_recv[0]
    else:
        shared = jnp.where(iota((ROWS, 128), 1) < EDGE, z_recv[1], z_recv[0])
    spread_sum = dot_nn(stacked(shared), spread)
    grid_ref[...] = partial + spread_sum[:ROWS] + spread_sum[ROWS:]

    rows_of = {1: pl.ds(ROWS - 8, 8), -1: pl.ds(0, 8), 0: pl.ds(0, ROWS)}
    lanes_of = {1: pl.ds(LANES - 128, 128), -1: pl.ds(0, 128), 0: pl.ds(0, LANES)}
    xy_copies = []
    landing = {}
    for slot, (i, j, _) in enumerate(xy_steps):
        if i and j:
            target = c_recv.at[(0 if i > 0 else 2) + (0 if j > 0 else 1)]
        elif i:
            target = x_recv.at[0 if i > 0 else 1]
        else:
            target = y_recv.at[0 if j > 0 else 1]
        landing[i, j] = target
        xy_copies.append(send(grid_ref.at[rows_of[i], lanes_of[j]], target, xy_sems, slot, (i, j, 0)))

    plan = plan_ref[...].astype(f32)
    cap = plan.shape[1]
    leaving = FACES * cap
    wide = jnp.concatenate(
        [jnp.broadcast_to(plan[q : q + 1], (cap, cap)) for q in range(FACES)], axis=0
    )
    diagonal = (iota((leaving, cap), 0) & (cap - 1)) == iota((leaving, cap), 1)
    chosen = jnp.sum(jnp.where(diagonal, wide, 0.0), axis=1, keepdims=True)
    picked = jnp.where(iota((leaving, count), 1).astype(f32) == chosen, 1.0, 0.0).astype(f32)
    taken = jnp.sum(picked, axis=0, keepdims=True)
    picker = jnp.concatenate([picked, jnp.zeros((128 - leaving, count), f32)], axis=0).astype(bf16)
    full = jnp.concatenate([record, anchor, living, jnp.zeros((2, count), f32)], axis=0)

    def thirds(value):
        high = value.astype(bf16).astype(f32)
        rest = value - high
        middle = rest.astype(bf16).astype(f32)
        return jnp.concatenate([high, middle, rest - middle], axis=0).astype(bf16)

    def pick(dot, value):
        got = dot(thirds(value), picker)
        return got[0:32] + got[32:64] + got[64:96]

    some = pick(dot_nt, full)
    some_tables = axis_tables(some[26:29], some[21:24])
    fill_tables(some_high, some_low, some_tables)

    for copy in xy_copies:
        copy.wait()
    near = iota((ROWS, 128), 1) < EDGE
    near8 = iota((8, 128), 1) < EDGE
    partial = grid_ref[...]
    low_side = y_recv[0]
    high_side = jnp.where(near, y_recv[1], 0.0)
    middle = jnp.zeros((8, LANES - 256), f32)
    low_rows = x_recv[0] + jnp.concatenate(
        [c_recv[0], middle, jnp.where(near8, c_recv[1], 0.0)], axis=1
    )
    high_rows = x_recv[1] + jnp.concatenate(
        [c_recv[2], middle, jnp.where(near8, c_recv[3], 0.0)], axis=1
    )
    totals = jnp.concatenate(
        [
            partial[:, 0:128] + low_side,
            partial[:, 128 : LANES - 128],
            partial[:, LANES - 128 :] + high_side,
        ],
        axis=1,
    )
    totals = jnp.concatenate(
        [totals[0:8] + low_rows, totals[8 : ROWS - 8], totals[ROWS - 8 :] + high_rows], axis=0
    )
    channel = iota((ROWS, LANES), 0) & 3
    mass_of = jnp.where(
        channel == 1,
        pltpu.roll(totals, 1, 0),
        jnp.where(channel == 2, pltpu.roll(totals, 2, 0), pltpu.roll(totals, 3, 0)),
    )
    velocity = totals / jnp.maximum(mass_of, mass_floor)
    velocity = jnp.where(channel == 3, velocity - time_step * gravity, velocity)
    velocity = jnp.where(channel == 0, 0.0, velocity)

    read_back(
        leave_ref, some, some[26:29], some[29:30], some_tables, some_high, some_low, velocity
    )
    m_steps = ((1, 0, 0), (-1, 0, 0), (0, 1, 0), (0, -1, 0)) + z_steps
    m_copies = [
        send(leave_ref, come_ref.at[slot], m_sems, slot, step) for slot, step in enumerate(m_steps)
    ]
    read_back(new_ref, record, anchor, living, tables, high_ref, low_ref, velocity)
    for copy in m_copies:
        copy.wait()
    face = jnp.right_shift(iota((32, 128), 1), cap.bit_length() - 1)
    come = come_ref[0]
    for q in range(1, FACES):
        come = jnp.where(face == q, come_ref[min(q, len(m_steps) - 1)], come)
    placed = pick(dot_nn, come)
    out_ref[...] = jnp.where(taken > 0.0, placed, new_ref[...])[0:26]


def body(sizes, particles, block_ids, node_offsets, live_count, migrations):
    count = particles.shape[1]
    vmem = pl.BlockSpec(memory_space=pltpu.VMEM)
    return pl.pallas_call(
        functools.partial(kernel, sizes),
        out_shape=jax.ShapeDtypeStruct(particles.shape, f32),
        in_specs=[pl.BlockSpec(memory_space=pltpu.SMEM)] + [vmem] * 4,
        out_specs=vmem,
        scratch_shapes=[
            pltpu.VMEM((LANES, 3 * count), bf16),
            pltpu.VMEM((LANES, 3 * count), bf16),
            pltpu.VMEM((128, 3 * count), bf16),
            pltpu.VMEM((128, 3 * count), bf16),
            pltpu.VMEM((LANES, 3 * 128), bf16),
            pltpu.VMEM((LANES, 3 * 128), bf16),
            pltpu.VMEM((ROWS, LANES), f32),
            pltpu.VMEM((ROWS, 128), f32),
            pltpu.VMEM((2, ROWS, 128), f32),
            pltpu.VMEM((2, 8, LANES), f32),
            pltpu.VMEM((2, ROWS, 128), f32),
            pltpu.VMEM((4, 8, 128), f32),
            pltpu.VMEM((32, 128), f32),
            pltpu.VMEM((FACES, 32, 128), f32),
            pltpu.VMEM((32, count), f32),
            pltpu.SemaphoreType.DMA((2, 2)),
            pltpu.SemaphoreType.DMA((2, 8)),
            pltpu.SemaphoreType.DMA((2, 6)),
        ],
        compiler_params=pltpu.CompilerParams(
            collective_id=0, has_side_effects=True, vmem_limit_bytes=32 * 1024 * 1024
        ),
        name="substep",
    )(
        live_count,
        particles,
        block_ids.reshape(1, count),
        node_offsets.reshape(1, count),
        migrations,
    )


def solution(mesh):
    sizes = tuple(mesh.shape[name] for name in AXES)
    return jax.shard_map(
        functools.partial(body, sizes),
        mesh=mesh,
        in_specs=(
            P(None, AXES),
            P(AXES),
            P(AXES),
            P(AXES),
            P(None, AXES),
        ),
        out_specs=P(None, AXES),
        check_vma=False,
    )
```

time: 80.4 us -> 23.6 us (0.29)
  starting transfers between devices: 24.6 us -> 0 us
  Pallas kernels: 0 us -> 19.8 us
  waiting for transfers between devices: 16.3 us -> 0 us
  matrix products: 13.5 us -> 0 us
  other arithmetic: 10.5 us -> 0 us
  local copies, waits for them, and re-layouts: 13.1 us -> 2.85 us
  between operations: 2.04 us -> 0.68 us
    ppermute x18 -> x0, starting transfers between devices: 24.6 us -> none  [the longest x9 16.4 us: extended_2(): lax.ppermute(lax.slice_in_dim(block, 0, width, axis=dim), axis, backward)]
    pallas_call x0 -> x1, Pallas kernels: none -> 19.8 us  [body(): pl.pallas_call(functools.partial(kernel, sizes), out_shape=jax.ShapeDtype...]
    ppermute x18 -> x0, waiting for transfers between devices: 16.3 us -> none  [the longest x9 11.2 us: extended_2(): lax.ppermute(lax.slice_in_dim(block, block.shape[dim] - width, None, axis...]
    dot_general x8 -> x0, matrix products: 13.5 us -> none  [the longest x4 6.85 us: contract_inner(): lax.dot_general(left_side, right_side, (((1,), (0,)), ((), ())), precisio...]
    concatenate x8 -> x0, other arithmetic: 5.52 us -> none  [the longest x4 4.95 us: extended_2(): block = jnp.concatenate([low, block, high], axis=dim)]
    slice x20 -> x0, local copies, waits for them, and re-layouts: 4.39 us -> none  [the longest x6 1.84 us: extended_2(): lax.slice_in_dim(block, block.shape[dim] - width, None, axis=dim)]
    ppermute x4 -> x0, local copies, waits for them, and re-layouts: 3.25 us -> none  [the longest x2 2.01 us: extended_2(): lax.ppermute(lax.slice_in_dim(block, 0, width, axis=dim), axis, backward)]
    unnamed x17 -> x9, local copies, waits for them, and re-layouts: 0.22 us -> 2.85 us
  transfers between devices with their start and end apart: 18 -> 0, of which waited for: 13 -> 0; matrix products, arithmetic and copies ran while one was open for 3% -> 0% of each run, Pallas kernels for 0% -> 0%
where the time goes in v1:
time: 23.6 us; the launch traced here: 23.3 us
  Pallas kernels  19.8 us (84%)
  local copies, waits for them, and re-layouts  2.85 us (12%)
  between operations  0.68 us (3%)
    pallas_call x1, Pallas kernels, body(): pl.pallas_call(functools.partial(kernel, sizes), out_shape=jax.ShapeDtype...  19.8 us
    unnamed x9, local copies, waits for them, and re-layouts  2.85 us

profile of v1, /device:TPU:0, one launch (start us, length us, event | category | flops | bytes accessed | tf_op | source)
XLA Modules:
  0.0 23.3 jit_solution(9266956288792308214)
XLA Ops:
  0.0 0.0 copy-start.1
  0.7 0.0 copy-done.1
  0.7 0.0 copy-start
  0.7 0.8 %copy-done = f32[26,512]{1,0:T(8,128)S(1)} copy-done((f32[26,512]{1,0:T(8,128)S(1)}, f32[26,512]{1,0:T(8,128)}, u32[]{:S(2)}) %copy-start) | copy-done | bytes 53272
  1.5 0.0 copy-start.2
  1.5 0.7 %copy-done.2 = s32[512]{0:T(512)S(1)} copy-done((s32[512]{0:T(512)S(1)}, s32[512]{0:T(512)}, u32[]{:S(2)}) %copy-start.2) | copy-done | bytes 2072
  2.2 0.0 copy-start.3
  2.2 0.7 %copy-done.3 = s32[512]{0:T(512)S(1)} copy-done((s32[512]{0:T(512)S(1)}, s32[512]{0:T(512)}, u32[]{:S(2)}) %copy-start.3) | copy-done | bytes 2072
  2.9 19.8 %substep.1 = f32[26,512]{1,0:T(8,128)S(1)} custom-call(s32[1]{0:T(128)S(6)} %copy.7.live_ref, f32[26,512]{1,0:T(8,128)S(1)} %copy-done, s32[1,512]{1,0:T(1,128)S(1)} %bitcast.2, s32[1,512]{1,0:T(1,128)S(1)} %bitcast.3, s32[6,8]{1,0:T(8,128)S(1)} %copy-done.1), custom_call_target="tpu_custom_call" | custom-call | tf_op jit(solution)/shard_map/substep/pallas_call | solution.py:422
  22.7 0.6 %copy.8 = f32[26,512]{1,0:T(8,128)} copy(f32[26,512]{1,0:T(8,128)S(1)} %substep.1) | data formatting | bytes 106496
Async XLA Ops:
  0.0 0.7 %copy-start.1 = (s32[6,8]{1,0:T(8,128)S(1)}, s32[6,8]{1,0:T(8,128)}, u32[]{:S(2)}) copy-start(s32[6,8]{1,0:T(8,128)} %plan_ref.1) | copy-start | bytes 580
  0.7 0.8 %copy-start = (f32[26,512]{1,0:T(8,128)S(1)}, f32[26,512]{1,0:T(8,128)}, u32[]{:S(2)}) copy-start(f32[26,512]{1,0:T(8,128)} %record_ref.1) | copy-start | bytes 159748
  1.5 0.7 %copy-start.2 = (s32[512]{0:T(512)S(1)}, s32[512]{0:T(512)}, u32[]{:S(2)}) copy-start(s32[512]{0:T(512)} %param.6) | copy-start | bytes 6148
  2.2 0.7 %copy-start.3 = (s32[512]{0:T(512)S(1)}, s32[512]{0:T(512)}, u32[]{:S(2)}) copy-start(s32[512]{0:T(512)} %param.7) | copy-start | bytes 6148

commit v2 on v1

--- a/solution.py
+++ b/solution.py
@@ -15,6 +15,7 @@
 LANES = 512
 USED = STRIDE * SPAN
 EDGE = 2 * STRIDE
+CENTRE = 0.5 * (SPAN - 1)
 FACES = 6
 
 time_step = 0.05
@@ -78,38 +79,39 @@
     )
 
 
-def store_pair(high_ref, low_ref, row, column, outer_line, inner_line, picks):
-    count = inner_line.shape[1]
+def store_pair(high_ref, low_ref, row, outer_line, inner_line, picks):
     pair = jnp.concatenate([outer_line[p : p + 1] * inner_line for p in picks], axis=0)
     high, low = split(pair)
-    high_ref[row : row + EDGE, column : column + count] = high
-    low_ref[row : row + EDGE, column : column + count] = low
+    high_ref[row : row + EDGE, :] = high
+    low_ref[row : row + EDGE, :] = low
 
 
 def fill_tables(high_ref, low_ref, tables):
-    _, (weight_y, shift_y), (weight_z, shift_z) = tables
+    _, (weight_y, _), (weight_z, _) = tables
     count = weight_y.shape[1]
-    for part, (outer, inner) in enumerate(
-        ((weight_y, weight_z), (shift_y, weight_z), (weight_y, shift_z))
-    ):
-        for pair in range(SPAN // 2):
-            store_pair(
-                high_ref, low_ref, EDGE * pair, part * count, outer, inner, (2 * pair, 2 * pair + 1)
-            )
+    for pair in range(SPAN // 2):
+        store_pair(high_ref, low_ref, EDGE * pair, weight_y, weight_z, (2 * pair, 2 * pair + 1))
     for ref in (high_ref, low_ref):
-        ref[USED:LANES, :] = jnp.zeros((LANES - USED, 3 * count), bf16)
+        ref[USED:LANES, :] = jnp.zeros((LANES - USED, count), bf16)
 
 
 def fill_face(high_ref, low_ref, tables):
-    _, (weight_y, shift_y), (weight_z, shift_z) = tables
+    _, (weight_y, _), (weight_z, _) = tables
     count = weight_y.shape[1]
-    for part, (outer, inner) in enumerate(
-        ((weight_z, weight_y), (weight_z, shift_y), (shift_z, weight_y))
-    ):
-        store_pair(high_ref, low_ref, 0, part * count, outer, inner, (0, 1))
-        store_pair(high_ref, low_ref, EDGE, part * count, outer, inner, (SPAN - 2, SPAN - 1))
+    store_pair(high_ref, low_ref, 0, weight_z, weight_y, (0, 1))
+    store_pair(high_ref, low_ref, EDGE, weight_z, weight_y, (SPAN - 2, SPAN - 1))
     for ref in (high_ref, low_ref):
-        ref[2 * EDGE : 128, :] = jnp.zeros((128 - 2 * EDGE, 3 * count), bf16)
+        ref[2 * EDGE : 128, :] = jnp.zeros((128 - 2 * EDGE, count), bf16)
+
+
+def lane_places(lanes):
+    lane = iota((1, lanes), 1)
+    line = jnp.right_shift(lane * 2731, 16)
+    return line.astype(f32) - CENTRE, (lane - STRIDE * line).astype(f32) - CENTRE
+
+
+def combine(parts, place_y, place_z):
+    return parts[:ROWS] + place_y * parts[ROWS : 2 * ROWS] + place_z * parts[2 * ROWS :]
 
 
 def product(left, right):
@@ -170,12 +172,13 @@
             total = total + value[row : row + 8]
         return total[0:4] + total[4:8]
 
-    first = reads[:, 0:count]
+    first = reads[:ROWS]
     speed = fold(weight_x * first) * living
+    place = anchor + record[21:24] - CENTRE
     along = [
         4.0 * living * fold(shift_x * first),
-        4.0 * living * fold(weight_x * reads[:, count : 2 * count]),
-        4.0 * living * fold(weight_x * reads[:, 2 * count : 3 * count]),
+        4.0 * (living * fold(weight_x * reads[ROWS : 2 * ROWS]) - place[1:2] * speed),
+        4.0 * (living * fold(weight_x * reads[2 * ROWS :]) - place[2:3] * speed),
     ]
     out_ref[0:3, :] = speed[1:4]
     deform = [record[12 + 3 * k : 15 + 3 * k] for k in range(3)]
@@ -193,12 +196,18 @@
 
 def kernel(
     sizes,
+    live_hbm,
+    record_hbm,
+    block_hbm,
+    offset_hbm,
+    plan_hbm,
+    out_ref,
     live_ref,
     record_ref,
     block_ref,
     offset_ref,
     plan_ref,
-    out_ref,
+    in_sems,
     high_ref,
     low_ref,
     face_high,
@@ -218,6 +227,19 @@
     xy_sems,
     m_sems,
 ):
+    operands = (
+        (record_hbm, record_ref),
+        (block_hbm, block_ref),
+        (offset_hbm, offset_ref),
+        (live_hbm, live_ref),
+        (plan_hbm, plan_ref),
+    )
+    in_copies = [
+        pltpu.make_async_copy(source, target, in_sems.at[slot])
+        for slot, (source, target) in enumerate(operands)
+    ]
+    for copy in in_copies:
+        copy.start()
     me = [lax.axis_index(name) for name in AXES]
 
     def at(*step):
@@ -232,6 +254,8 @@
     for step in z_steps + xy_steps:
         pl.semaphore_signal(barrier, inc=1, device_id=at(*step), device_id_type=MESH)
 
+    for copy in in_copies:
+        copy.wait()
     count = record_ref.shape[1]
     record = record_ref[...]
     fraction = record[21:24]
@@ -266,19 +290,30 @@
         for i in range(3)
     ]
     none = jnp.zeros((1, count), f32)
-    base = jnp.concatenate([held, held * record[0:3]] * 2, axis=0)
+    places = anchor + fraction - CENTRE
+    momentum = [
+        held * record[i : i + 1] - coupling[i][1] * places[1:2] - coupling[i][2] * places[2:3]
+        for i in range(3)
+    ]
+    base = jnp.concatenate([held] + momentum + [held] + momentum, axis=0)
     pushes = [
         jnp.concatenate([none, coupling[0][j], coupling[1][j], coupling[2][j]] * 2, axis=0)
         for j in range(3)
     ]
     weight_x, shift_x = tables[0]
     tiles = range(0, ROWS, 8)
-    first = [base * weight_x[r : r + 8] + pushes[0] * shift_x[r : r + 8] for r in tiles]
-    second = [pushes[1] * weight_x[r : r + 8] for r in tiles]
-    third = [pushes[2] * weight_x[r : r + 8] for r in tiles]
-    left = jnp.concatenate([jnp.concatenate(part, axis=0) for part in (first, second, third)], axis=1)
-
-    z_send[...] = contract(dot_nt, left, face_high[...], face_low[...])
+    left = jnp.concatenate(
+        [base * weight_x[r : r + 8] + pushes[0] * shift_x[r : r + 8] for r in tiles]
+        + [pushes[1] * weight_x[r : r + 8] for r in tiles]
+        + [pushes[2] * weight_x[r : r + 8] for r in tiles],
+        axis=0,
+    )
+
+    face_lane = iota((1, 128), 1)
+    face_k = jnp.right_shift(face_lane * 2731, 16)
+    face_y = (face_lane - STRIDE * face_k).astype(f32) - CENTRE
+    face_z = jnp.where(face_k < 2, face_k, face_k + (SPAN - 4)).astype(f32) - CENTRE
+    z_send[...] = combine(contract(dot_nt, left, face_high[...], face_low[...]), face_y, face_z)
     pl.semaphore_wait(barrier, len(z_steps) + len(xy_steps))
 
     def send(source, target, sems, slot, step):
@@ -298,18 +333,19 @@
     ]
 
     fill_tables(high_ref, low_ref, tables)
-    partial = contract(dot_nt, left, high_ref[...], low_ref[...])
+    lane_y, lane_z = lane_places(LANES)
+    partial = combine(contract(dot_nt, left, high_ref[...], low_ref[...]), lane_y, lane_z)
 
     lane = iota((128, LANES), 1)
     row = iota((128, LANES), 0)
-    lane_y = jnp.right_shift(lane * 2731, 16)
+    line = jnp.right_shift(lane * 2731, 16)
     row_k = jnp.right_shift(row * 2731, 16)
     goal_z = jnp.where(row_k < 2, row_k + (SPAN - 2), row_k - 2)
     spread = jnp.where(
-        (row - STRIDE * row_k == lane_y)
-        & (lane - STRIDE * lane_y == goal_z)
+        (row - STRIDE * row_k == line)
+        & (lane - STRIDE * line == goal_z)
         & (row_k < 4)
-        & (lane_y < SPAN),
+        & (line < SPAN),
         1.0,
         0.0,
     ).astype(bf16)
@@ -397,6 +433,7 @@
     velocity = totals / jnp.maximum(mass_of, mass_floor)
     velocity = jnp.where(channel == 3, velocity - time_step * gravity, velocity)
     velocity = jnp.where(channel == 0, 0.0, velocity)
+    velocity = jnp.concatenate([velocity, velocity * lane_y, velocity * lane_z], axis=0)
 
     read_back(
         leave_ref, some, some[26:29], some[29:30], some_tables, some_high, some_low, velocity
@@ -422,15 +459,21 @@
     return pl.pallas_call(
         functools.partial(kernel, sizes),
         out_shape=jax.ShapeDtypeStruct(particles.shape, f32),
-        in_specs=[pl.BlockSpec(memory_space=pltpu.SMEM)] + [vmem] * 4,
+        in_specs=[pl.BlockSpec(memory_space=pltpu.HBM)] * 5,
         out_specs=vmem,
         scratch_shapes=[
-            pltpu.VMEM((LANES, 3 * count), bf16),
-            pltpu.VMEM((LANES, 3 * count), bf16),
-            pltpu.VMEM((128, 3 * count), bf16),
-            pltpu.VMEM((128, 3 * count), bf16),
-            pltpu.VMEM((LANES, 3 * 128), bf16),
-            pltpu.VMEM((LANES, 3 * 128), bf16),
+            pltpu.SMEM((1,), jnp.int32),
+            pltpu.VMEM(particles.shape, f32),
+            pltpu.VMEM((1, count), jnp.int32),
+            pltpu.VMEM((1, count), jnp.int32),
+            pltpu.VMEM(migrations.shape, jnp.int32),
+            pltpu.SemaphoreType.DMA((5,)),
+            pltpu.VMEM((LANES, count), bf16),
+            pltpu.VMEM((LANES, count), bf16),
+            pltpu.VMEM((128, count), bf16),
+            pltpu.VMEM((128, count), bf16),
+            pltpu.VMEM((LANES, 128), bf16),
+            pltpu.VMEM((LANES, 128), bf16),
             pltpu.VMEM((ROWS, LANES), f32),
             pltpu.VMEM((ROWS, 128), f32),
             pltpu.VMEM((2, ROWS, 128), f32),
@@ -445,7 +488,7 @@
             pltpu.SemaphoreType.DMA((2, 6)),
         ],
         compiler_params=pltpu.CompilerParams(
-            collective_id=0, has_side_effects=True, vmem_limit_bytes=32 * 1024 * 1024
+            collective_id=0, has_side_effects=True, vmem_limit_bytes=60 * 1024 * 1024
         ),
         name="substep",
     )(

time: 23.6 us -> 22.4 us (0.949)
  local copies, waits for them, and re-layouts: 2.85 us -> 1.47 us
  Pallas kernels: 19.8 us -> 20.1 us
    unnamed x9 -> x1, local copies, waits for them, and re-layouts: 2.85 us -> 1.47 us
where the time goes in v2:
time: 22.4 us; the launch traced here: 22.2 us
  Pallas kernels  20.1 us (90%)
  local copies, waits for them, and re-layouts  1.47 us (7%)
  between operations  0.66 us (3%)
    pallas_call x1, Pallas kernels, body(): pl.pallas_call(functools.partial(kernel, sizes), out_shape=jax.ShapeDtype...  20.1 us
    unnamed x1, local copies, waits for them, and re-layouts  1.47 us

profile of v2, /device:TPU:0, one launch (start us, length us, event | category | flops | bytes accessed | tf_op | source)
XLA Modules:
  0.0 22.2 jit_solution(1057293300487833494)
XLA Ops:
  0.7 20.1 %substep.1 = f32[26,512]{1,0:T(8,128)} custom-call(s32[1]{0:T(128)S(6)} %copy.7.live_hbm, f32[26,512]{1,0:T(8,128)} %record_hbm.1, s32[1,512]{1,0:T(1,128)} %bitcast.2, s32[1,512]{1,0:T(1,128)} %bitcast.3, s32[6,8]{1,0:T(8,128)} %plan_hbm.1), custom_call_target="tpu_custom_call" | custom-call | tf_op jit(solution)/shard_map/substep/pallas_call | solution.py:459
  20.7 1.5 %copy.8 = f32[26,512]{1,0:T(8,128)} copy(f32[26,512]{1,0:T(8,128)} %substep.1) | data formatting | bytes 106496

commit v3 on v2

--- a/solution.py
+++ b/solution.py
@@ -15,6 +15,7 @@
 LANES = 512
 USED = STRIDE * SPAN
 EDGE = 2 * STRIDE
+FOLD = 40
 CENTRE = 0.5 * (SPAN - 1)
 FACES = 6
 
@@ -192,6 +193,22 @@
     out_ref[21:24, :] = record[21:24] * living + time_step * speed[1:4]
     out_ref[24:26, :] = record[24:26] * living
     out_ref[26:32, :] = jnp.zeros((6, count), f32)
+
+
+def pack_side(tile):
+    rest = jnp.concatenate([tile[FOLD:], jnp.zeros((2 * FOLD - ROWS, 128), f32)], axis=0)
+    return jnp.where(iota((FOLD, 128), 1) < 64, tile[:FOLD], pltpu.roll(rest, 64, 1))
+
+
+def open_side(packed):
+    rest = pltpu.roll(packed, 64, 1)[: ROWS - FOLD]
+    full = jnp.concatenate([packed, rest], axis=0)
+    return jnp.where(iota((ROWS, 128), 1) < EDGE, full, 0.0)
+
+
+def turned(value):
+    rows = jnp.zeros((128 - value.shape[0], 128), f32)
+    return jnp.concatenate([value, rows], axis=0).T
 
 
 def kernel(
@@ -218,9 +235,11 @@
     z_send,
     z_recv,
     x_recv,
+    y_send,
     y_recv,
     c_recv,
     leave_ref,
+    m_send,
     come_ref,
     new_ref,
     z_sems,
@@ -249,7 +268,7 @@
 
     pair_z = sizes[2] == 2
     z_steps = ((0, 0, 1),) if pair_z else ((0, 0, 1), (0, 0, -1))
-    xy_steps = tuple((i, j, 0) for i in (1, 0, -1) for j in (1, 0, -1) if i or j)
+    xy_steps = tuple((i, j, 0) for i in (0, 1, -1) for j in (1, -1, 0) if i or j)
     barrier = pltpu.get_barrier_semaphore()
     for step in z_steps + xy_steps:
         pl.semaphore_signal(barrier, inc=1, device_id=at(*step), device_id_type=MESH)
@@ -356,21 +375,25 @@
     else:
         shared = jnp.where(iota((ROWS, 128), 1) < EDGE, z_recv[1], z_recv[0])
     spread_sum = dot_nn(stacked(shared), spread)
-    grid_ref[...] = partial + spread_sum[:ROWS] + spread_sum[ROWS:]
-
-    rows_of = {1: pl.ds(ROWS - 8, 8), -1: pl.ds(0, 8), 0: pl.ds(0, ROWS)}
-    lanes_of = {1: pl.ds(LANES - 128, 128), -1: pl.ds(0, 128), 0: pl.ds(0, LANES)}
+    partial = partial + spread_sum[:ROWS] + spread_sum[ROWS:]
+    grid_ref[...] = partial
+    y_send[0] = pack_side(partial[:, LANES - 128 :])
+    y_send[1] = pack_side(partial[:, 0:128])
+
+    rows_of = {1: pl.ds(ROWS - 8, 8), -1: pl.ds(0, 8)}
+    lanes_of = {1: pl.ds(LANES - 128, 128), -1: pl.ds(0, 128)}
     xy_copies = []
-    landing = {}
     for slot, (i, j, _) in enumerate(xy_steps):
         if i and j:
+            source = grid_ref.at[rows_of[i], lanes_of[j]]
             target = c_recv.at[(0 if i > 0 else 2) + (0 if j > 0 else 1)]
         elif i:
+            source = grid_ref.at[rows_of[i], :]
             target = x_recv.at[0 if i > 0 else 1]
         else:
+            source = y_send.at[0 if j > 0 else 1]
             target = y_recv.at[0 if j > 0 else 1]
-        landing[i, j] = target
-        xy_copies.append(send(grid_ref.at[rows_of[i], lanes_of[j]], target, xy_sems, slot, (i, j, 0)))
+        xy_copies.append(send(source, target, xy_sems, slot, (i, j, 0)))
 
     plan = plan_ref[...].astype(f32)
     cap = plan.shape[1]
@@ -401,11 +424,10 @@
 
     for copy in xy_copies:
         copy.wait()
-    near = iota((ROWS, 128), 1) < EDGE
     near8 = iota((8, 128), 1) < EDGE
     partial = grid_ref[...]
-    low_side = y_recv[0]
-    high_side = jnp.where(near, y_recv[1], 0.0)
+    low_side = open_side(y_recv[0])
+    high_side = open_side(y_recv[1])
     middle = jnp.zeros((8, LANES - 256), f32)
     low_rows = x_recv[0] + jnp.concatenate(
         [c_recv[0], middle, jnp.where(near8, c_recv[1], 0.0)], axis=1
@@ -438,18 +460,16 @@
     read_back(
         leave_ref, some, some[26:29], some[29:30], some_tables, some_high, some_low, velocity
     )
-    m_steps = ((1, 0, 0), (-1, 0, 0), (0, 1, 0), (0, -1, 0)) + z_steps
+    m_send[...] = turned(leave_ref[...])[:leaving].reshape(FACES, cap, 128)
+    m_steps = ((1, 0, 0), (-1, 0, 0), (0, 1, 0), (0, -1, 0), (0, 0, 1), (0, 0, -1))
     m_copies = [
-        send(leave_ref, come_ref.at[slot], m_sems, slot, step) for slot, step in enumerate(m_steps)
+        send(m_send.at[slot], come_ref.at[slot], m_sems, slot, step)
+        for slot, step in enumerate(m_steps)
     ]
     read_back(new_ref, record, anchor, living, tables, high_ref, low_ref, velocity)
     for copy in m_copies:
         copy.wait()
-    face = jnp.right_shift(iota((32, 128), 1), cap.bit_length() - 1)
-    come = come_ref[0]
-    for q in range(1, FACES):
-        come = jnp.where(face == q, come_ref[min(q, len(m_steps) - 1)], come)
-    placed = pick(dot_nn, come)
+    placed = pick(dot_nn, turned(come_ref[...].reshape(leaving, 128))[:32])
     out_ref[...] = jnp.where(taken > 0.0, placed, new_ref[...])[0:26]
 
 
@@ -458,7 +478,7 @@
     vmem = pl.BlockSpec(memory_space=pltpu.VMEM)
     return pl.pallas_call(
         functools.partial(kernel, sizes),
-        out_shape=jax.ShapeDtypeStruct(particles.shape, f32),
+        out_shape=pltpu.VMEM(particles.shape, f32),
         in_specs=[pl.BlockSpec(memory_space=pltpu.HBM)] * 5,
         out_specs=vmem,
         scratch_shapes=[
@@ -478,10 +498,12 @@
             pltpu.VMEM((ROWS, 128), f32),
             pltpu.VMEM((2, ROWS, 128), f32),
             pltpu.VMEM((2, 8, LANES), f32),
-            pltpu.VMEM((2, ROWS, 128), f32),
+            pltpu.VMEM((2, FOLD, 128), f32),
+            pltpu.VMEM((2, FOLD, 128), f32),
             pltpu.VMEM((4, 8, 128), f32),
             pltpu.VMEM((32, 128), f32),
-            pltpu.VMEM((FACES, 32, 128), f32),
+            pltpu.VMEM((FACES, migrations.shape[1], 128), f32),
+            pltpu.VMEM((FACES, migrations.shape[1], 128), f32),
             pltpu.VMEM((32, count), f32),
             pltpu.SemaphoreType.DMA((2, 2)),
             pltpu.SemaphoreType.DMA((2, 8)),

time: 22.4 us -> 20.1 us (0.90)
  Pallas kernels: 20.1 us -> 18.7 us
  local copies, waits for them, and re-layouts: 1.47 us -> 0.63 us
    pallas_call x1, Pallas kernels: 20.1 us -> 18.7 us  [body(): pl.pallas_call(functools.partial(kernel, sizes), out_shape=pltpu.VMEM(par...]
    unnamed x1, local copies, waits for them, and re-layouts: 1.47 us -> 0.63 us
where the time goes in v3:
time: 20.1 us; the launch traced here: 20 us
  Pallas kernels  18.7 us (93%)
  between operations  0.66 us (3%)
  local copies, waits for them, and re-layouts  0.63 us (3%)
    pallas_call x1, Pallas kernels, body(): pl.pallas_call(functools.partial(kernel, sizes), out_shape=pltpu.VMEM(par...  18.7 us
    unnamed x1, local copies, waits for them, and re-layouts  0.63 us

profile of v3, /device:TPU:0, one launch (start us, length us, event | category | flops | bytes accessed | tf_op | source)
XLA Modules:
  0.0 20.0 jit_solution(4963758159249564208)
XLA Ops:
  0.7 18.7 %substep.1 = f32[26,512]{1,0:T(8,128)S(1)} custom-call(s32[1]{0:T(128)S(6)} %copy.8.live_hbm, f32[26,512]{1,0:T(8,128)} %record_hbm.1, s32[1,512]{1,0:T(1,128)} %bitcast.2, s32[1,512]{1,0:T(1,128)} %bitcast.3, s32[6,8]{1,0:T(8,128)} %plan_hbm.1), custom_call_target="tpu_custom_call" | custom-call | tf_op jit(solution)/shard_map/substep/pallas_call | solution.py:479
  19.3 0.6 %copy.7 = f32[26,512]{1,0:T(8,128)} copy(f32[26,512]{1,0:T(8,128)S(1)} %substep.1) | data formatting | bytes 106496

commit v4 on v3

--- a/solution.py
+++ b/solution.py
@@ -96,13 +96,29 @@
         ref[USED:LANES, :] = jnp.zeros((LANES - USED, count), bf16)
 
 
-def fill_face(high_ref, low_ref, tables):
-    _, (weight_y, _), (weight_z, _) = tables
-    count = weight_y.shape[1]
-    store_pair(high_ref, low_ref, 0, weight_z, weight_y, (0, 1))
-    store_pair(high_ref, low_ref, EDGE, weight_z, weight_y, (SPAN - 2, SPAN - 1))
-    for ref in (high_ref, low_ref):
-        ref[2 * EDGE : 128, :] = jnp.zeros((128 - 2 * EDGE, count), bf16)
+def fill_masks(gather_ref, spread_ref):
+    lane = iota((128, LANES), 1)
+    row = iota((128, LANES), 0)
+    line = jnp.right_shift(lane * 2731, 16)
+    place = lane - STRIDE * line
+    k = row & 3
+    same = (jnp.right_shift(row, 2) == line) & (line < SPAN)
+    near = jnp.where(k < 2, k, k + (SPAN - 4))
+    far = jnp.where(k < 2, k + (SPAN - 2), k - 2)
+    gather_ref[...] = jnp.where(same & (place == near), 1.0, 0.0).astype(bf16)
+    spread_ref[...] = jnp.where(same & (place == far), 1.0, 0.0).astype(bf16)
+
+
+def pack_edges(face):
+    group = jnp.right_shift(iota((8, 128), 1), 3)
+    tiles = []
+    for start in (4 * (SPAN - 2), 0):
+        tile = jnp.zeros((8, 128), f32)
+        for g in range(ROWS // 8):
+            rolled = pltpu.roll(face[8 * g : 8 * g + 8], (8 * g - start) % 128, 1)
+            tile = jnp.where(group == g, rolled, tile)
+        tiles.append(tile)
+    return tiles
 
 
 def lane_places(lanes):
@@ -227,13 +243,15 @@
     in_sems,
     high_ref,
     low_ref,
-    face_high,
-    face_low,
+    gather_ref,
+    spread_ref,
     some_high,
     some_low,
     grid_ref,
     z_send,
     z_recv,
+    e_send,
+    e_recv,
     x_recv,
     y_send,
     y_recv,
@@ -270,9 +288,11 @@
     z_steps = ((0, 0, 1),) if pair_z else ((0, 0, 1), (0, 0, -1))
     xy_steps = tuple((i, j, 0) for i in (0, 1, -1) for j in (1, -1, 0) if i or j)
     barrier = pltpu.get_barrier_semaphore()
-    for step in z_steps + xy_steps:
+    around = xy_steps + tuple((i, j, k) for _, _, k in z_steps for i, j, _ in ((0, 0, 0),) + xy_steps)
+    for step in around:
         pl.semaphore_signal(barrier, inc=1, device_id=at(*step), device_id_type=MESH)
 
+    fill_masks(gather_ref, spread_ref)
     for copy in in_copies:
         copy.wait()
     count = record_ref.shape[1]
@@ -294,7 +314,7 @@
     living = jnp.where(iota((1, count), 1) < live_ref[0], 1.0, 0.0).astype(f32)
 
     tables = axis_tables(anchor, fraction)
-    fill_face(face_high, face_low, tables)
+    fill_tables(high_ref, low_ref, tables)
 
     plastic = pack(record[25:26])
     deform = [[pack(record[12 + 3 * i + j : 13 + 3 * i + j]) for j in range(3)] for i in range(3)]
@@ -328,13 +348,6 @@
         axis=0,
     )
 
-    face_lane = iota((1, 128), 1)
-    face_k = jnp.right_shift(face_lane * 2731, 16)
-    face_y = (face_lane - STRIDE * face_k).astype(f32) - CENTRE
-    face_z = jnp.where(face_k < 2, face_k, face_k + (SPAN - 4)).astype(f32) - CENTRE
-    z_send[...] = combine(contract(dot_nt, left, face_high[...], face_low[...]), face_y, face_z)
-    pl.semaphore_wait(barrier, len(z_steps) + len(xy_steps))
-
     def send(source, target, sems, slot, step):
         copy = pltpu.make_async_remote_copy(
             src_ref=source,
@@ -347,38 +360,12 @@
         copy.start()
         return copy
 
-    z_copies = [
-        send(z_send, z_recv.at[slot], z_sems, slot, step) for slot, step in enumerate(z_steps)
-    ]
-
-    fill_tables(high_ref, low_ref, tables)
     lane_y, lane_z = lane_places(LANES)
     partial = combine(contract(dot_nt, left, high_ref[...], low_ref[...]), lane_y, lane_z)
-
-    lane = iota((128, LANES), 1)
-    row = iota((128, LANES), 0)
-    line = jnp.right_shift(lane * 2731, 16)
-    row_k = jnp.right_shift(row * 2731, 16)
-    goal_z = jnp.where(row_k < 2, row_k + (SPAN - 2), row_k - 2)
-    spread = jnp.where(
-        (row - STRIDE * row_k == line)
-        & (lane - STRIDE * line == goal_z)
-        & (row_k < 4)
-        & (line < SPAN),
-        1.0,
-        0.0,
-    ).astype(bf16)
-    for copy in z_copies:
-        copy.wait()
-    if pair_z:
-        shared = z_recv[0]
-    else:
-        shared = jnp.where(iota((ROWS, 128), 1) < EDGE, z_recv[1], z_recv[0])
-    spread_sum = dot_nn(stacked(shared), spread)
-    partial = partial + spread_sum[:ROWS] + spread_sum[ROWS:]
     grid_ref[...] = partial
     y_send[0] = pack_side(partial[:, LANES - 128 :])
     y_send[1] = pack_side(partial[:, 0:128])
+    pl.semaphore_wait(barrier, len(around))
 
     rows_of = {1: pl.ds(ROWS - 8, 8), -1: pl.ds(0, 8)}
     lanes_of = {1: pl.ds(LANES - 128, 128), -1: pl.ds(0, 128)}
@@ -395,6 +382,18 @@
             target = y_recv.at[0 if j > 0 else 1]
         xy_copies.append(send(source, target, xy_sems, slot, (i, j, 0)))
 
+    face = dot_nt(stacked(partial), gather_ref[...])
+    face = face[:ROWS] + face[ROWS:]
+    z_send[...] = face
+    e_send[0], e_send[1] = pack_edges(face)
+    z_copies = []
+    for slot, (_, _, k) in enumerate(z_steps):
+        z_copies.append(send(z_send, z_recv.at[slot], z_sems, 9 * slot, (0, 0, k)))
+        for number, (i, j, _) in enumerate(xy_steps):
+            source = z_send.at[rows_of[i]] if i else e_send.at[0 if j > 0 else 1]
+            target = e_recv.at[slot, number]
+            z_copies.append(send(source, target, z_sems, 9 * slot + 1 + number, (i, j, k)))
+
     plan = plan_ref[...].astype(f32)
     cap = plan.shape[1]
     leaving = FACES * cap
@@ -422,10 +421,37 @@
     some_tables = axis_tables(some[26:29], some[21:24])
     fill_tables(some_high, some_low, some_tables)
 
+    for copy in z_copies:
+        copy.wait()
+
+    def from_z(ref, *index):
+        if pair_z:
+            return ref[(0,) + index]
+        value = ref[(1,) + index]
+        return jnp.where((iota(value.shape, 1) & 3) < 2, value, ref[(0,) + index])
+
+    face_lane = iota((8, 128), 1)
+    face_side = {1: face_lane < 8, -1: (face_lane >= 4 * (SPAN - 2)) & (face_lane < 4 * SPAN)}
+    face_start = {1: 0, -1: 4 * (SPAN - 2)}
+    edge = {(i, j): from_z(e_recv, number) for number, (i, j, _) in enumerate(xy_steps)}
+    shared = from_z(z_recv)
+    shared = [shared[8 * g : 8 * g + 8] for g in range(ROWS // 8)]
+    for g in range(ROWS // 8):
+        for j in (1, -1):
+            rolled = pltpu.roll(edge[0, j], (face_start[j] - 8 * g) % 128, 1)
+            shared[g] = jnp.where(face_side[j], shared[g] + rolled, shared[g])
+    for i in (1, -1):
+        g = 0 if i > 0 else ROWS // 8 - 1
+        shared[g] = shared[g] + edge[i, 0]
+        for j in (1, -1):
+            rolled = pltpu.roll(edge[i, j], (face_start[j] - face_start[-j]) % 128, 1)
+            shared[g] = jnp.where(face_side[j], shared[g] + rolled, shared[g])
+    spread_sum = dot_nn(stacked(jnp.concatenate(shared, axis=0)), spread_ref[...])
+    partial = grid_ref[...] + spread_sum[:ROWS] + spread_sum[ROWS:]
+
     for copy in xy_copies:
         copy.wait()
     near8 = iota((8, 128), 1) < EDGE
-    partial = grid_ref[...]
     low_side = open_side(y_recv[0])
     high_side = open_side(y_recv[1])
     middle = jnp.zeros((8, LANES - 256), f32)
@@ -490,13 +516,15 @@
             pltpu.SemaphoreType.DMA((5,)),
             pltpu.VMEM((LANES, count), bf16),
             pltpu.VMEM((LANES, count), bf16),
-            pltpu.VMEM((128, count), bf16),
-            pltpu.VMEM((128, count), bf16),
+            pltpu.VMEM((128, LANES), bf16),
+            pltpu.VMEM((128, LANES), bf16),
             pltpu.VMEM((LANES, 128), bf16),
             pltpu.VMEM((LANES, 128), bf16),
             pltpu.VMEM((ROWS, LANES), f32),
             pltpu.VMEM((ROWS, 128), f32),
             pltpu.VMEM((2, ROWS, 128), f32),
+            pltpu.VMEM((2, 8, 128), f32),
+            pltpu.VMEM((2, 8, 8, 128), f32),
             pltpu.VMEM((2, 8, LANES), f32),
             pltpu.VMEM((2, FOLD, 128), f32),
             pltpu.VMEM((2, FOLD, 128), f32),
@@ -505,7 +533,7 @@
             pltpu.VMEM((FACES, migrations.shape[1], 128), f32),
             pltpu.VMEM((FACES, migrations.shape[1], 128), f32),
             pltpu.VMEM((32, count), f32),
-            pltpu.SemaphoreType.DMA((2, 2)),
+            pltpu.SemaphoreType.DMA((2, 18)),
             pltpu.SemaphoreType.DMA((2, 8)),
             pltpu.SemaphoreType.DMA((2, 6)),
         ],

time: 20.1 us -> 18.4 us (0.915)
  Pallas kernels: 18.7 us -> 16.9 us
    pallas_call x1, Pallas kernels: 18.7 us -> 16.9 us  [body(): pl.pallas_call(functools.partial(kernel, sizes), out_shape=pltpu.VMEM(par...]
where the time goes in v4:
time: 18.4 us; the launch traced here: 18.2 us
  Pallas kernels  16.9 us (92%)
  between operations  0.66 us (4%)
  local copies, waits for them, and re-layouts  0.63 us (3%)
    pallas_call x1, Pallas kernels, body(): pl.pallas_call(functools.partial(kernel, sizes), out_shape=pltpu.VMEM(par...  16.9 us
    unnamed x1, local copies, waits for them, and re-layouts  0.63 us

profile of v4, /device:TPU:0, one launch (start us, length us, event | category | flops | bytes accessed | tf_op | source)
XLA Modules:
  0.0 18.2 jit_solution(8656909096647639713)
XLA Ops:
  0.7 16.9 %substep.1 = f32[26,512]{1,0:T(8,128)S(1)} custom-call(s32[1]{0:T(128)S(6)} %copy.8.live_hbm, f32[26,512]{1,0:T(8,128)} %record_hbm.1, s32[1,512]{1,0:T(1,128)} %bitcast.2, s32[1,512]{1,0:T(1,128)} %bitcast.3, s32[6,8]{1,0:T(8,128)} %plan_hbm.1), custom_call_target="tpu_custom_call" | custom-call | tf_op jit(solution)/shard_map/substep/pallas_call | solution.py:505
  17.6 0.6 %copy.7 = f32[26,512]{1,0:T(8,128)} copy(f32[26,512]{1,0:T(8,128)S(1)} %substep.1) | data formatting | bytes 106496

commit v5 on v4

--- a/solution.py
+++ b/solution.py
@@ -15,7 +15,10 @@
 LANES = 512
 USED = STRIDE * SPAN
 EDGE = 2 * STRIDE
-FOLD = 40
+SIDE = STRIDE + SPAN
+THIRD = ROWS // 3
+HEAD = 40
+FACE_ROWS = HEAD + 8
 CENTRE = 0.5 * (SPAN - 1)
 FACES = 6
 
@@ -212,14 +215,64 @@
 
 
 def pack_side(tile):
-    rest = jnp.concatenate([tile[FOLD:], jnp.zeros((2 * FOLD - ROWS, 128), f32)], axis=0)
-    return jnp.where(iota((FOLD, 128), 1) < 64, tile[:FOLD], pltpu.roll(rest, 64, 1))
+    lane = iota((THIRD, 128), 1)
+    middle = pltpu.roll(tile[THIRD : 2 * THIRD], SIDE, 1)
+    last = pltpu.roll(tile[2 * THIRD :], 2 * SIDE, 1)
+    return jnp.where(lane < SIDE, tile[:THIRD], jnp.where(lane < 2 * SIDE, middle, last))
 
 
 def open_side(packed):
-    rest = pltpu.roll(packed, 64, 1)[: ROWS - FOLD]
-    full = jnp.concatenate([packed, rest], axis=0)
-    return jnp.where(iota((ROWS, 128), 1) < EDGE, full, 0.0)
+    rolled = [packed] + [pltpu.roll(packed, 128 - g * SIDE, 1) for g in (1, 2)]
+    return jnp.where(iota((ROWS, 128), 1) < SIDE, jnp.concatenate(rolled, axis=0), 0.0)
+
+
+def pack_corner(tile):
+    return jnp.where(iota((4, 128), 1) < 64, tile[0:4], pltpu.roll(tile[4:8], 64, 1))
+
+
+def open_corner(packed):
+    full = jnp.concatenate([packed, pltpu.roll(packed, 64, 1)], axis=0)
+    return jnp.where(iota((8, 128), 1) < SIDE, full, 0.0)
+
+
+def pack_face(face):
+    rest = jnp.concatenate([face[HEAD:], jnp.zeros((2 * HEAD - ROWS, 128), f32)], axis=0)
+    head = jnp.where(iota((HEAD, 128), 1) < 72, face[:HEAD], pltpu.roll(rest, 72, 1))
+    group = jnp.right_shift(iota((8, 128), 1), 4)
+    tail = jnp.zeros((8, 128), f32)
+    for g in range((ROWS - HEAD) // 8):
+        rolled = pltpu.roll(rest[8 * g : 8 * g + 8], (16 * g - 56) % 128, 1)
+        tail = jnp.where(group == g, rolled, tail)
+    return jnp.concatenate([head, tail], axis=0)
+
+
+def open_face(packed):
+    tiles = [packed[r : r + 8] for r in range(0, HEAD, 8)]
+    tail = packed[HEAD:]
+    lane = iota((8, 128), 1)
+    for g in range((ROWS - HEAD) // 8):
+        body_part = pltpu.roll(packed[8 * g : 8 * g + 8], 56, 1)
+        tiles.append(jnp.where(lane < 56, body_part, pltpu.roll(tail, (56 - 16 * g) % 128, 1)))
+    return tiles
+
+
+def pack_line(tile, start):
+    group = jnp.right_shift(iota((8, 128), 1), 3)
+    row = iota((8, 128), 0)
+    total = jnp.zeros((8, 128), f32)
+    for r in range(8):
+        rolled = pltpu.roll(tile, (8 * r - start) % 128, 1)
+        total = jnp.where((group == r) & (row == r), rolled, total)
+    return jnp.sum(total, axis=0, keepdims=True)
+
+
+def open_line(packed, start):
+    wide = jnp.broadcast_to(packed, (8, 128))
+    row = iota((8, 128), 0)
+    total = pltpu.roll(wide, start, 1) if start else wide
+    for r in range(1, 8):
+        total = jnp.where(row == r, pltpu.roll(wide, (start - 8 * r) % 128, 1), total)
+    return total
 
 
 def turned(value):
@@ -255,7 +308,10 @@
     x_recv,
     y_send,
     y_recv,
+    c_send,
     c_recv,
+    l_send,
+    l_recv,
     leave_ref,
     m_send,
     come_ref,
@@ -367,32 +423,52 @@
     y_send[1] = pack_side(partial[:, 0:128])
     pl.semaphore_wait(barrier, len(around))
 
-    rows_of = {1: pl.ds(ROWS - 8, 8), -1: pl.ds(0, 8)}
-    lanes_of = {1: pl.ds(LANES - 128, 128), -1: pl.ds(0, 128)}
+    corners = ((1, 1), (1, -1), (-1, 1), (-1, -1))
+    sides = ((0, 1), (0, -1), (1, 0), (-1, 0))
+    last = {1: ROWS - 8, -1: 0}
+    last_lane = {1: LANES - 128, -1: 0}
+    last_face = {1: 4 * (SPAN - 2), -1: 0}
+    for number, (i, j) in enumerate(corners):
+        c_send[number] = pack_corner(
+            partial[last[i] : last[i] + 8, last_lane[j] : last_lane[j] + 128]
+        )
     xy_copies = []
     for slot, (i, j, _) in enumerate(xy_steps):
         if i and j:
-            source = grid_ref.at[rows_of[i], lanes_of[j]]
-            target = c_recv.at[(0 if i > 0 else 2) + (0 if j > 0 else 1)]
+            number = corners.index((i, j))
+            source, target = c_send.at[number], c_recv.at[number]
         elif i:
-            source = grid_ref.at[rows_of[i], :]
+            source = grid_ref.at[pl.ds(last[i], 8), :]
             target = x_recv.at[0 if i > 0 else 1]
         else:
-            source = y_send.at[0 if j > 0 else 1]
-            target = y_recv.at[0 if j > 0 else 1]
+            number = 0 if j > 0 else 1
+            source, target = y_send.at[number], y_recv.at[number]
         xy_copies.append(send(source, target, xy_sems, slot, (i, j, 0)))
 
     face = dot_nt(stacked(partial), gather_ref[...])
     face = face[:ROWS] + face[ROWS:]
-    z_send[...] = face
+    z_send[...] = pack_face(face)
+    z_copies = [
+        send(z_send, z_recv.at[slot], z_sems, 9 * slot, (0, 0, k))
+        for slot, (_, _, k) in enumerate(z_steps)
+    ]
     e_send[0], e_send[1] = pack_edges(face)
-    z_copies = []
+    e_send[2] = face[last[1] : last[1] + 8]
+    e_send[3] = face[last[-1] : last[-1] + 8]
     for slot, (_, _, k) in enumerate(z_steps):
-        z_copies.append(send(z_send, z_recv.at[slot], z_sems, 9 * slot, (0, 0, k)))
-        for number, (i, j, _) in enumerate(xy_steps):
-            source = z_send.at[rows_of[i]] if i else e_send.at[0 if j > 0 else 1]
+        for number, (i, j) in enumerate(sides):
             target = e_recv.at[slot, number]
-            z_copies.append(send(source, target, z_sems, 9 * slot + 1 + number, (i, j, k)))
+            z_copies.append(
+                send(e_send.at[number], target, z_sems, 9 * slot + 1 + number, (i, j, k))
+            )
+    for number, (i, j) in enumerate(corners):
+        l_send[number] = pack_line(face[last[i] : last[i] + 8], last_face[j])
+    for slot, (_, _, k) in enumerate(z_steps):
+        for number, (i, j) in enumerate(corners):
+            target = l_recv.at[slot, number]
+            z_copies.append(
+                send(l_send.at[number], target, z_sems, 9 * slot + 5 + number, (i, j, k))
+            )
 
     plan = plan_ref[...].astype(f32)
     cap = plan.shape[1]
@@ -433,9 +509,8 @@
     face_lane = iota((8, 128), 1)
     face_side = {1: face_lane < 8, -1: (face_lane >= 4 * (SPAN - 2)) & (face_lane < 4 * SPAN)}
     face_start = {1: 0, -1: 4 * (SPAN - 2)}
-    edge = {(i, j): from_z(e_recv, number) for number, (i, j, _) in enumerate(xy_steps)}
-    shared = from_z(z_recv)
-    shared = [shared[8 * g : 8 * g + 8] for g in range(ROWS // 8)]
+    edge = {step: from_z(e_recv, number) for number, step in enumerate(sides)}
+    shared = open_face(from_z(z_recv))
     for g in range(ROWS // 8):
         for j in (1, -1):
             rolled = pltpu.roll(edge[0, j], (face_start[j] - 8 * g) % 128, 1)
@@ -444,23 +519,19 @@
         g = 0 if i > 0 else ROWS // 8 - 1
         shared[g] = shared[g] + edge[i, 0]
         for j in (1, -1):
-            rolled = pltpu.roll(edge[i, j], (face_start[j] - face_start[-j]) % 128, 1)
-            shared[g] = jnp.where(face_side[j], shared[g] + rolled, shared[g])
+            line = open_line(from_z(l_recv, corners.index((i, j))), face_start[j])
+            shared[g] = jnp.where(face_side[j], shared[g] + line, shared[g])
     spread_sum = dot_nn(stacked(jnp.concatenate(shared, axis=0)), spread_ref[...])
     partial = grid_ref[...] + spread_sum[:ROWS] + spread_sum[ROWS:]
 
     for copy in xy_copies:
         copy.wait()
-    near8 = iota((8, 128), 1) < EDGE
     low_side = open_side(y_recv[0])
     high_side = open_side(y_recv[1])
     middle = jnp.zeros((8, LANES - 256), f32)
-    low_rows = x_recv[0] + jnp.concatenate(
-        [c_recv[0], middle, jnp.where(near8, c_recv[1], 0.0)], axis=1
-    )
-    high_rows = x_recv[1] + jnp.concatenate(
-        [c_recv[2], middle, jnp.where(near8, c_recv[3], 0.0)], axis=1
-    )
+    corner = [open_corner(c_recv[number]) for number in range(4)]
+    low_rows = x_recv[0] + jnp.concatenate([corner[0], middle, corner[1]], axis=1)
+    high_rows = x_recv[1] + jnp.concatenate([corner[2], middle, corner[3]], axis=1)
     totals = jnp.concatenate(
         [
             partial[:, 0:128] + low_side,
@@ -521,14 +592,17 @@
             pltpu.VMEM((LANES, 128), bf16),
             pltpu.VMEM((LANES, 128), bf16),
             pltpu.VMEM((ROWS, LANES), f32),
-            pltpu.VMEM((ROWS, 128), f32),
-            pltpu.VMEM((2, ROWS, 128), f32),
-            pltpu.VMEM((2, 8, 128), f32),
-            pltpu.VMEM((2, 8, 8, 128), f32),
+            pltpu.VMEM((FACE_ROWS, 128), f32),
+            pltpu.VMEM((2, FACE_ROWS, 128), f32),
+            pltpu.VMEM((4, 8, 128), f32),
+            pltpu.VMEM((2, 4, 8, 128), f32),
             pltpu.VMEM((2, 8, LANES), f32),
-            pltpu.VMEM((2, FOLD, 128), f32),
-            pltpu.VMEM((2, FOLD, 128), f32),
-            pltpu.VMEM((4, 8, 128), f32),
+            pltpu.VMEM((2, THIRD, 128), f32),
+            pltpu.VMEM((2, THIRD, 128), f32),
+            pltpu.VMEM((4, 4, 128), f32),
+            pltpu.VMEM((4, 4, 128), f32),
+            pltpu.VMEM((4, 1, 128), f32),
+            pltpu.VMEM((2, 4, 1, 128), f32),
             pltpu.VMEM((32, 128), f32),
             pltpu.VMEM((FACES, migrations.shape[1], 128), f32),
             pltpu.VMEM((FACES, migrations.shape[1], 128), f32),

time: 18.4 us -> 17.6 us (0.957)
  Pallas kernels: 16.9 us -> 16.2 us
    pallas_call x1, Pallas kernels: 16.9 us -> 16.2 us  [body(): pl.pallas_call(functools.partial(kernel, sizes), out_shape=pltpu.VMEM(par...]
where the time goes in v5:
time: 17.6 us; the launch traced here: 17.5 us
  Pallas kernels  16.2 us (92%)
  between operations  0.66 us (4%)
  local copies, waits for them, and re-layouts  0.63 us (4%)
    pallas_call x1, Pallas kernels, body(): pl.pallas_call(functools.partial(kernel, sizes), out_shape=pltpu.VMEM(par...  16.2 us
    unnamed x1, local copies, waits for them, and re-layouts  0.63 us

profile of v5, /device:TPU:0, one launch (start us, length us, event | category | flops | bytes accessed | tf_op | source)
XLA Modules:
  0.0 17.5 jit_solution(2188459126502222690)
XLA Ops:
  0.7 16.2 %substep.1 = f32[26,512]{1,0:T(8,128)S(1)} custom-call(s32[1]{0:T(128)S(6)} %copy.8.live_hbm, f32[26,512]{1,0:T(8,128)} %record_hbm.1, s32[1,512]{1,0:T(1,128)} %bitcast.2, s32[1,512]{1,0:T(1,128)} %bitcast.3, s32[6,8]{1,0:T(8,128)} %plan_hbm.1), custom_call_target="tpu_custom_call" | custom-call | tf_op jit(solution)/shard_map/substep/pallas_call | solution.py:576
  16.8 0.6 %copy.7 = f32[26,512]{1,0:T(8,128)} copy(f32[26,512]{1,0:T(8,128)S(1)} %substep.1) | data formatting | bytes 106496

commit v6 on v5

--- a/solution.py
+++ b/solution.py
@@ -90,16 +90,17 @@
     low_ref[row : row + EDGE, :] = low
 
 
-def fill_tables(high_ref, low_ref, tables):
+def fill_tables(high_ref, low_ref, tables, pairs=range(SPAN // 2)):
     _, (weight_y, _), (weight_z, _) = tables
     count = weight_y.shape[1]
-    for pair in range(SPAN // 2):
+    for pair in pairs:
         store_pair(high_ref, low_ref, EDGE * pair, weight_y, weight_z, (2 * pair, 2 * pair + 1))
-    for ref in (high_ref, low_ref):
-        ref[USED:LANES, :] = jnp.zeros((LANES - USED, count), bf16)
-
-
-def fill_masks(gather_ref, spread_ref):
+    if len(pairs) == SPAN // 2:
+        for ref in (high_ref, low_ref):
+            ref[USED:LANES, :] = jnp.zeros((LANES - USED, count), bf16)
+
+
+def fill_masks(gather_ref, spread_ref, corner_ref):
     lane = iota((128, LANES), 1)
     row = iota((128, LANES), 0)
     line = jnp.right_shift(lane * 2731, 16)
@@ -109,6 +110,11 @@
     near = jnp.where(k < 2, k, k + (SPAN - 4))
     far = jnp.where(k < 2, k + (SPAN - 2), k - 2)
     gather_ref[...] = jnp.where(same & (place == near), 1.0, 0.0).astype(bf16)
+    corner_ref[...] = jnp.where(
+        jnp.where(line < 2, line, line + (SPAN - 4)) == jnp.right_shift(row, 2),
+        jnp.where((place == near) & (line < 4), 1.0, 0.0),
+        0.0,
+    )[:, :128].astype(bf16)
     spread_ref[...] = jnp.where(same & (place == far), 1.0, 0.0).astype(bf16)
 
 
@@ -298,6 +304,7 @@
     low_ref,
     gather_ref,
     spread_ref,
+    corner_ref,
     some_high,
     some_low,
     grid_ref,
@@ -348,7 +355,7 @@
     for step in around:
         pl.semaphore_signal(barrier, inc=1, device_id=at(*step), device_id_type=MESH)
 
-    fill_masks(gather_ref, spread_ref)
+    fill_masks(gather_ref, spread_ref, corner_ref)
     for copy in in_copies:
         copy.wait()
     count = record_ref.shape[1]
@@ -370,7 +377,7 @@
     living = jnp.where(iota((1, count), 1) < live_ref[0], 1.0, 0.0).astype(f32)
 
     tables = axis_tables(anchor, fraction)
-    fill_tables(high_ref, low_ref, tables)
+    fill_tables(high_ref, low_ref, tables, (0, SPAN // 2 - 1))
 
     plastic = pack(record[25:26])
     deform = [[pack(record[12 + 3 * i + j : 13 + 3 * i + j]) for j in range(3)] for i in range(3)]
@@ -416,53 +423,48 @@
         copy.start()
         return copy
 
-    lane_y, lane_z = lane_places(LANES)
-    partial = combine(contract(dot_nt, left, high_ref[...], low_ref[...]), lane_y, lane_z)
-    grid_ref[...] = partial
-    y_send[0] = pack_side(partial[:, LANES - 128 :])
-    y_send[1] = pack_side(partial[:, 0:128])
-    pl.semaphore_wait(barrier, len(around))
-
     corners = ((1, 1), (1, -1), (-1, 1), (-1, -1))
     sides = ((0, 1), (0, -1), (1, 0), (-1, 0))
     last = {1: ROWS - 8, -1: 0}
-    last_lane = {1: LANES - 128, -1: 0}
     last_face = {1: 4 * (SPAN - 2), -1: 0}
+
+    blank = jnp.zeros((128 - 2 * EDGE, count), bf16)
+    edge_high, edge_low = [
+        jnp.concatenate([ref[0:EDGE, :], ref[USED - EDGE : USED, :], blank], axis=0)
+        for ref in (high_ref, low_ref)
+    ]
+    lane_y, lane_z = lane_places(128)
+    lane_y = jnp.where(lane_y < 2 - CENTRE, lane_y, lane_y + (SPAN - 4))
+    ends = combine(contract(dot_nt, left, edge_high, edge_low), lane_y, lane_z)
+    ends = {-1: ends, 1: pltpu.roll(ends, 128 - EDGE, 1)}
+    y_send[0] = pack_side(ends[1])
+    y_send[1] = pack_side(ends[-1])
     for number, (i, j) in enumerate(corners):
-        c_send[number] = pack_corner(
-            partial[last[i] : last[i] + 8, last_lane[j] : last_lane[j] + 128]
-        )
+        c_send[number] = pack_corner(ends[j][last[i] : last[i] + 8])
+    pl.semaphore_wait(barrier, len(around))
     xy_copies = []
-    for slot, (i, j, _) in enumerate(xy_steps):
-        if i and j:
-            number = corners.index((i, j))
-            source, target = c_send.at[number], c_recv.at[number]
-        elif i:
-            source = grid_ref.at[pl.ds(last[i], 8), :]
-            target = x_recv.at[0 if i > 0 else 1]
-        else:
-            number = 0 if j > 0 else 1
-            source, target = y_send.at[number], y_recv.at[number]
-        xy_copies.append(send(source, target, xy_sems, slot, (i, j, 0)))
-
-    face = dot_nt(stacked(partial), gather_ref[...])
+    for number, j in enumerate((1, -1)):
+        xy_copies.append(send(y_send.at[number], y_recv.at[number], xy_sems, number, (0, j, 0)))
+    for number, (i, j) in enumerate(corners):
+        xy_copies.append(send(c_send.at[number], c_recv.at[number], xy_sems, 2 + number, (i, j, 0)))
+
+    face = dot_nt(stacked(ends[-1]), corner_ref[...])
     face = face[:ROWS] + face[ROWS:]
-    z_send[...] = pack_face(face)
-    z_copies = [
-        send(z_send, z_recv.at[slot], z_sems, 9 * slot, (0, 0, k))
-        for slot, (_, _, k) in enumerate(z_steps)
-    ]
     e_send[0], e_send[1] = pack_edges(face)
-    e_send[2] = face[last[1] : last[1] + 8]
-    e_send[3] = face[last[-1] : last[-1] + 8]
-    for slot, (_, _, k) in enumerate(z_steps):
-        for number, (i, j) in enumerate(sides):
-            target = e_recv.at[slot, number]
-            z_copies.append(
-                send(e_send.at[number], target, z_sems, 9 * slot + 1 + number, (i, j, k))
-            )
     for number, (i, j) in enumerate(corners):
         l_send[number] = pack_line(face[last[i] : last[i] + 8], last_face[j])
+    z_copies = []
+
+    def send_edges(numbers):
+        for slot, (_, _, k) in enumerate(z_steps):
+            for number in numbers:
+                i, j = sides[number]
+                target = e_recv.at[slot, number]
+                z_copies.append(
+                    send(e_send.at[number], target, z_sems, 9 * slot + 1 + number, (i, j, k))
+                )
+
+    send_edges((0, 1))
     for slot, (_, _, k) in enumerate(z_steps):
         for number, (i, j) in enumerate(corners):
             target = l_recv.at[slot, number]
@@ -470,6 +472,24 @@
                 send(l_send.at[number], target, z_sems, 9 * slot + 5 + number, (i, j, k))
             )
 
+    fill_tables(high_ref, low_ref, tables, range(1, SPAN // 2 - 1))
+    for ref in (high_ref, low_ref):
+        ref[USED:LANES, :] = jnp.zeros((LANES - USED, count), bf16)
+    lane_y, lane_z = lane_places(LANES)
+    partial = combine(contract(dot_nt, left, high_ref[...], low_ref[...]), lane_y, lane_z)
+    grid_ref[...] = partial
+    for number, i in enumerate((1, -1)):
+        source = grid_ref.at[pl.ds(last[i], 8), :]
+        xy_copies.append(send(source, x_recv.at[number], xy_sems, 6 + number, (i, 0, 0)))
+    face = dot_nt(stacked(partial), gather_ref[...])
+    face = face[:ROWS] + face[ROWS:]
+    z_send[...] = pack_face(face)
+    for slot, (_, _, k) in enumerate(z_steps):
+        z_copies.append(send(z_send, z_recv.at[slot], z_sems, 9 * slot, (0, 0, k)))
+    e_send[2] = face[last[1] : last[1] + 8]
+    e_send[3] = face[last[-1] : last[-1] + 8]
+    send_edges((2, 3))
+
     plan = plan_ref[...].astype(f32)
     cap = plan.shape[1]
     leaving = FACES * cap
@@ -498,7 +518,7 @@
     fill_tables(some_high, some_low, some_tables)
 
     for copy in z_copies:
-        copy.wait()
+        copy.wait_recv()
 
     def from_z(ref, *index):
         if pair_z:
@@ -525,7 +545,7 @@
     partial = grid_ref[...] + spread_sum[:ROWS] + spread_sum[ROWS:]
 
     for copy in xy_copies:
-        copy.wait()
+        copy.wait_recv()
     low_side = open_side(y_recv[0])
     high_side = open_side(y_recv[1])
     middle = jnp.zeros((8, LANES - 256), f32)
@@ -564,8 +584,10 @@
         for slot, step in enumerate(m_steps)
     ]
     read_back(new_ref, record, anchor, living, tables, high_ref, low_ref, velocity)
+    for copy in xy_copies + z_copies + m_copies:
+        copy.wait_send()
     for copy in m_copies:
-        copy.wait()
+        copy.wait_recv()
     placed = pick(dot_nn, turned(come_ref[...].reshape(leaving, 128))[:32])
     out_ref[...] = jnp.where(taken > 0.0, placed, new_ref[...])[0:26]
 
@@ -589,6 +611,7 @@
             pltpu.VMEM((LANES, count), bf16),
             pltpu.VMEM((128, LANES), bf16),
             pltpu.VMEM((128, LANES), bf16),
+            pltpu.VMEM((128, 128), bf16),
             pltpu.VMEM((LANES, 128), bf16),
             pltpu.VMEM((LANES, 128), bf16),
             pltpu.VMEM((ROWS, LANES), f32),

time: 17.6 us -> 17.5 us (level)
  no operation moved by 1% of the time
where the time goes in v6:
time: 17.5 us; the launch traced here: 17.4 us
  Pallas kernels  16.1 us (92%)
  between operations  0.66 us (4%)
  local copies, waits for them, and re-layouts  0.63 us (4%)
    pallas_call x1, Pallas kernels, body(): pl.pallas_call(functools.partial(kernel, sizes), out_shape=pltpu.VMEM(par...  16.1 us
    unnamed x1, local copies, waits for them, and re-layouts  0.63 us

profile of v6, /device:TPU:0, one launch (start us, length us, event | category | flops | bytes accessed | tf_op | source)
XLA Modules:
  0.0 17.4 jit_solution(1828504720980242888)
XLA Ops:
  0.7 16.1 %substep.1 = f32[26,512]{1,0:T(8,128)S(1)} custom-call(s32[1]{0:T(128)S(6)} %copy.8.live_hbm, f32[26,512]{1,0:T(8,128)} %record_hbm.1, s32[1,512]{1,0:T(1,128)} %bitcast.2, s32[1,512]{1,0:T(1,128)} %bitcast.3, s32[6,8]{1,0:T(8,128)} %plan_hbm.1), custom_call_target="tpu_custom_call" | custom-call | tf_op jit(solution)/shard_map/substep/pallas_call | solution.py:598
  16.7 0.6 %copy.7 = f32[26,512]{1,0:T(8,128)} copy(f32[26,512]{1,0:T(8,128)S(1)} %substep.1) | data formatting | bytes 106496

commit v7 on v6

--- a/solution.py
+++ b/solution.py
@@ -377,7 +377,10 @@
     living = jnp.where(iota((1, count), 1) < live_ref[0], 1.0, 0.0).astype(f32)
 
     tables = axis_tables(anchor, fraction)
-    fill_tables(high_ref, low_ref, tables, (0, SPAN // 2 - 1))
+    early = (0, 1, 2, SPAN // 2 - 1)
+    fill_tables(high_ref, low_ref, tables, early)
+    for ref in (high_ref, low_ref):
+        ref[USED:LANES, :] = jnp.zeros((LANES - USED, count), bf16)
 
     plastic = pack(record[25:26])
     deform = [[pack(record[12 + 3 * i + j : 13 + 3 * i + j]) for j in range(3)] for i in range(3)]
@@ -428,15 +431,23 @@
     last = {1: ROWS - 8, -1: 0}
     last_face = {1: 4 * (SPAN - 2), -1: 0}
 
-    blank = jnp.zeros((128 - 2 * EDGE, count), bf16)
-    edge_high, edge_low = [
-        jnp.concatenate([ref[0:EDGE, :], ref[USED - EDGE : USED, :], blank], axis=0)
-        for ref in (high_ref, low_ref)
-    ]
-    lane_y, lane_z = lane_places(128)
-    lane_y = jnp.where(lane_y < 2 - CENTRE, lane_y, lane_y + (SPAN - 4))
-    ends = combine(contract(dot_nt, left, edge_high, edge_low), lane_y, lane_z)
-    ends = {-1: ends, 1: pltpu.roll(ends, 128 - EDGE, 1)}
+    lane_y, lane_z = lane_places(LANES)
+    cut = LANES - 128
+
+    def outside(value, axis):
+        low, high = lax.slice_in_dim(value, 0, 128, axis=axis), lax.slice_in_dim(value, cut, LANES, axis=axis)
+        return jnp.concatenate([low, high], axis=axis)
+
+    ends = combine(
+        contract(
+            dot_nt,
+            left,
+            *[jnp.concatenate([ref[0:128, :], ref[cut:, :]], axis=0) for ref in (high_ref, low_ref)],
+        ),
+        outside(lane_y, 1),
+        outside(lane_z, 1),
+    )
+    ends = {-1: ends[:, :128], 1: ends[:, 128:]}
     y_send[0] = pack_side(ends[1])
     y_send[1] = pack_side(ends[-1])
     for number, (i, j) in enumerate(corners):
@@ -448,7 +459,8 @@
     for number, (i, j) in enumerate(corners):
         xy_copies.append(send(c_send.at[number], c_recv.at[number], xy_sems, 2 + number, (i, j, 0)))
 
-    face = dot_nt(stacked(ends[-1]), corner_ref[...])
+    both = jnp.where(iota((ROWS, 128), 1) < EDGE, ends[-1], pltpu.roll(ends[1], EDGE, 1))
+    face = dot_nt(stacked(both), corner_ref[...])
     face = face[:ROWS] + face[ROWS:]
     e_send[0], e_send[1] = pack_edges(face)
     for number, (i, j) in enumerate(corners):
@@ -472,11 +484,13 @@
                 send(l_send.at[number], target, z_sems, 9 * slot + 5 + number, (i, j, k))
             )
 
-    fill_tables(high_ref, low_ref, tables, range(1, SPAN // 2 - 1))
-    for ref in (high_ref, low_ref):
-        ref[USED:LANES, :] = jnp.zeros((LANES - USED, count), bf16)
-    lane_y, lane_z = lane_places(LANES)
-    partial = combine(contract(dot_nt, left, high_ref[...], low_ref[...]), lane_y, lane_z)
+    fill_tables(high_ref, low_ref, tables, range(3, SPAN // 2 - 1))
+    inside = combine(
+        contract(dot_nt, left, high_ref[128:cut, :], low_ref[128:cut, :]),
+        lane_y[:, 128:cut],
+        lane_z[:, 128:cut],
+    )
+    partial = jnp.concatenate([ends[-1], inside, ends[1]], axis=1)
     grid_ref[...] = partial
     for number, i in enumerate((1, -1)):
         source = grid_ref.at[pl.ds(last[i], 8), :]
@@ -517,6 +531,26 @@
     some_tables = axis_tables(some[26:29], some[21:24])
     fill_tables(some_high, some_low, some_tables)
 
+    for copy in xy_copies:
+        copy.wait_recv()
+    partial = grid_ref[...]
+    low_side = open_side(y_recv[0])
+    high_side = open_side(y_recv[1])
+    middle = jnp.zeros((8, LANES - 256), f32)
+    corner = [open_corner(c_recv[number]) for number in range(4)]
+    low_rows = x_recv[0] + jnp.concatenate([corner[0], middle, corner[1]], axis=1)
+    high_rows = x_recv[1] + jnp.concatenate([corner[2], middle, corner[3]], axis=1)
+    totals = jnp.concatenate(
+        [
+            partial[:, 0:128] + low_side,
+            partial[:, 128 : LANES - 128],
+            partial[:, LANES - 128 :] + high_side,
+        ],
+        axis=1,
+    )
+    totals = jnp.concatenate(
+        [totals[0:8] + low_rows, totals[8 : ROWS - 8], totals[ROWS - 8 :] + high_rows], axis=0
+    )
     for copy in z_copies:
         copy.wait_recv()
 
@@ -542,27 +576,8 @@
             line = open_line(from_z(l_recv, corners.index((i, j))), face_start[j])
             shared[g] = jnp.where(face_side[j], shared[g] + line, shared[g])
     spread_sum = dot_nn(stacked(jnp.concatenate(shared, axis=0)), spread_ref[...])
-    partial = grid_ref[...] + spread_sum[:ROWS] + spread_sum[ROWS:]
-
-    for copy in xy_copies:
-        copy.wait_recv()
-    low_side = open_side(y_recv[0])
-    high_side = open_side(y_recv[1])
-    middle = jnp.zeros((8, LANES - 256), f32)
-    corner = [open_corner(c_recv[number]) for number in range(4)]
-    low_rows = x_recv[0] + jnp.concatenate([corner[0], middle, corner[1]], axis=1)
-    high_rows = x_recv[1] + jnp.concatenate([corner[2], middle, corner[3]], axis=1)
-    totals = jnp.concatenate(
-        [
-            partial[:, 0:128] + low_side,
-            partial[:, 128 : LANES - 128],
-            partial[:, LANES - 128 :] + high_side,
-        ],
-        axis=1,
-    )
-    totals = jnp.concatenate(
-        [totals[0:8] + low_rows, totals[8 : ROWS - 8], totals[ROWS - 8 :] + high_rows], axis=0
-    )
+    totals = totals + spread_sum[:ROWS] + spread_sum[ROWS:]
+
     channel = iota((ROWS, LANES), 0) & 3
     mass_of = jnp.where(
         channel == 1,

time: 17.5 us -> 17.5 us (level)
  no operation moved by 1% of the time
where the time goes in v7:
time: 17.5 us; the launch traced here: 17.3 us
  Pallas kernels  16 us (91%)
  between operations  0.66 us (4%)
  local copies, waits for them, and re-layouts  0.63 us (4%)
    pallas_call x1, Pallas kernels, body(): pl.pallas_call(functools.partial(kernel, sizes), out_shape=pltpu.VMEM(par...  16 us
    unnamed x1, local copies, waits for them, and re-layouts  0.63 us

profile of v7, /device:TPU:0, one launch (start us, length us, event | category | flops | bytes accessed | tf_op | source)
XLA Modules:
  0.0 17.3 jit_solution(15288745074620784960)
XLA Ops:
  0.7 16.0 %substep.1 = f32[26,512]{1,0:T(8,128)S(1)} custom-call(s32[1]{0:T(128)S(6)} %copy.8.live_hbm, f32[26,512]{1,0:T(8,128)} %record_hbm.1, s32[1,512]{1,0:T(1,128)} %bitcast.2, s32[1,512]{1,0:T(1,128)} %bitcast.3, s32[6,8]{1,0:T(8,128)} %plan_hbm.1), custom_call_target="tpu_custom_call" | custom-call | tf_op jit(solution)/shard_map/substep/pallas_call | solution.py:613
  16.7 0.6 %copy.7 = f32[26,512]{1,0:T(8,128)} copy(f32[26,512]{1,0:T(8,128)S(1)} %substep.1) | data formatting | bytes 106496

commit v8 on v7

--- a/solution.py
+++ b/solution.py
@@ -90,14 +90,13 @@
     low_ref[row : row + EDGE, :] = low
 
 
-def fill_tables(high_ref, low_ref, tables, pairs=range(SPAN // 2)):
+def fill_tables(high_ref, low_ref, tables):
     _, (weight_y, _), (weight_z, _) = tables
     count = weight_y.shape[1]
-    for pair in pairs:
+    for pair in range(SPAN // 2):
         store_pair(high_ref, low_ref, EDGE * pair, weight_y, weight_z, (2 * pair, 2 * pair + 1))
-    if len(pairs) == SPAN // 2:
-        for ref in (high_ref, low_ref):
-            ref[USED:LANES, :] = jnp.zeros((LANES - USED, count), bf16)
+    for ref in (high_ref, low_ref):
+        ref[USED:LANES, :] = jnp.zeros((LANES - USED, count), bf16)
 
 
 def fill_masks(gather_ref, spread_ref, corner_ref):
@@ -377,10 +376,7 @@
     living = jnp.where(iota((1, count), 1) < live_ref[0], 1.0, 0.0).astype(f32)
 
     tables = axis_tables(anchor, fraction)
-    early = (0, 1, 2, SPAN // 2 - 1)
-    fill_tables(high_ref, low_ref, tables, early)
-    for ref in (high_ref, low_ref):
-        ref[USED:LANES, :] = jnp.zeros((LANES - USED, count), bf16)
+    fill_tables(high_ref, low_ref, tables)
 
     plastic = pack(record[25:26])
     deform = [[pack(record[12 + 3 * i + j : 13 + 3 * i + j]) for j in range(3)] for i in range(3)]
@@ -484,7 +480,6 @@
                 send(l_send.at[number], target, z_sems, 9 * slot + 5 + number, (i, j, k))
             )
 
-    fill_tables(high_ref, low_ref, tables, range(3, SPAN // 2 - 1))
     inside = combine(
         contract(dot_nt, left, high_ref[128:cut, :], low_ref[128:cut, :]),
         lane_y[:, 128:cut],

time: 17.5 us -> 17.5 us (level)
  no operation moved by 1% of the time
where the time goes in v8:
time: 17.5 us; the launch traced here: 17.3 us
  Pallas kernels  16 us (91%)
  between operations  0.66 us (4%)
  local copies, waits for them, and re-layouts  0.63 us (4%)
    pallas_call x1, Pallas kernels, body(): pl.pallas_call(functools.partial(kernel, sizes), out_shape=pltpu.VMEM(par...  16 us
    unnamed x1, local copies, waits for them, and re-layouts  0.63 us

profile of v8, /device:TPU:0, one launch (start us, length us, event | category | flops | bytes accessed | tf_op | source)
XLA Modules:
  0.0 17.3 jit_solution(17038353475735920074)
XLA Ops:
  0.7 16.0 %substep.1 = f32[26,512]{1,0:T(8,128)S(1)} custom-call(s32[1]{0:T(128)S(6)} %copy.8.live_hbm, f32[26,512]{1,0:T(8,128)} %record_hbm.1, s32[1,512]{1,0:T(1,128)} %bitcast.2, s32[1,512]{1,0:T(1,128)} %bitcast.3, s32[6,8]{1,0:T(8,128)} %plan_hbm.1), custom_call_target="tpu_custom_call" | custom-call | tf_op jit(solution)/shard_map/substep/pallas_call | solution.py:608
  16.7 0.6 %copy.7 = f32[26,512]{1,0:T(8,128)} copy(f32[26,512]{1,0:T(8,128)S(1)} %substep.1) | data formatting | bytes 106496

commit v9 on v8

--- a/solution.py
+++ b/solution.py
@@ -512,15 +512,9 @@
     picker = jnp.concatenate([picked, jnp.zeros((128 - leaving, count), f32)], axis=0).astype(bf16)
     full = jnp.concatenate([record, anchor, living, jnp.zeros((2, count), f32)], axis=0)
 
-    def thirds(value):
-        high = value.astype(bf16).astype(f32)
-        rest = value - high
-        middle = rest.astype(bf16).astype(f32)
-        return jnp.concatenate([high, middle, rest - middle], axis=0).astype(bf16)
-
     def pick(dot, value):
-        got = dot(thirds(value), picker)
-        return got[0:32] + got[32:64] + got[64:96]
+        got = dot(stacked(value), picker)
+        return got[0:32] + got[32:64]
 
     some = pick(dot_nt, full)
     some_tables = axis_tables(some[26:29], some[21:24])
@@ -591,7 +585,7 @@
     m_steps = ((1, 0, 0), (-1, 0, 0), (0, 1, 0), (0, -1, 0), (0, 0, 1), (0, 0, -1))
     m_copies = [
         send(m_send.at[slot], come_ref.at[slot], m_sems, slot, step)
-        for slot, step in enumerate(m_steps)
+        for slot, step in sorted(enumerate(m_steps), key=lambda pair: pair[1][1] == 0)
     ]
     read_back(new_ref, record, anchor, living, tables, high_ref, low_ref, velocity)
     for copy in xy_copies + z_copies + m_copies:

time: 17.5 us -> 17.5 us (level)
  no operation moved by 1% of the time
where the time goes in v9:
time: 17.5 us; the launch traced here: 17.3 us
  Pallas kernels  16 us (91%)
  between operations  0.66 us (4%)
  local copies, waits for them, and re-layouts  0.63 us (4%)
    pallas_call x1, Pallas kernels, body(): pl.pallas_call(functools.partial(kernel, sizes), out_shape=pltpu.VMEM(par...  16 us
    unnamed x1, local copies, waits for them, and re-layouts  0.63 us

profile of v9, /device:TPU:0, one launch (start us, length us, event | category | flops | bytes accessed | tf_op | source)
XLA Modules:
  0.0 17.3 jit_solution(4242881121503099521)
XLA Ops:
  0.7 16.0 %substep.1 = f32[26,512]{1,0:T(8,128)S(1)} custom-call(s32[1]{0:T(128)S(6)} %copy.8.live_hbm, f32[26,512]{1,0:T(8,128)} %record_hbm.1, s32[1,512]{1,0:T(1,128)} %bitcast.2, s32[1,512]{1,0:T(1,128)} %bitcast.3, s32[6,8]{1,0:T(8,128)} %plan_hbm.1), custom_call_target="tpu_custom_call" | custom-call | tf_op jit(solution)/shard_map/substep/pallas_call | solution.py:602
  16.7 0.6 %copy.7 = f32[26,512]{1,0:T(8,128)} copy(f32[26,512]{1,0:T(8,128)S(1)} %substep.1) | data formatting | bytes 106496
